TPU v7x, 32 devices: a whole 2x2x4 slice. The times are simulated.
32 devices in a mesh: segment: 4 (over y, x), wide: 8 (over z, core).
Axes of the slice: x: 2, y: 2, z: 4, core: 2. Of those that a mesh axis runs over, the one named last changes fastest.
Arguments:
- entering_hidden: bfloat16 [2, 16, 8192], P(None, 'wide'), may hold values from -6 to 6
- row_adapter_index: int32 [2, 16, 1], P(None, 'wide'), may hold values from 0 to 7; in each aligned block of 16 rows (0 to 15, 16 to 31, ..., all dimensions but the last counted through in order) at most 4 rows name the same one
- lengths: int32 [2, 16], P(None, 'wide'), may hold values from 2 to 384
- input_norm_gain: bfloat16 [4, 8192], P('segment'), may hold values from 0.099609375 to 1.8984375
- query_matrix: bfloat16 [4, 8192, 8192], P('segment', None, 'wide'), may hold values from -0.0625 to 0.0625
- key_matrix: bfloat16 [4, 8192, 1024], P('segment', None, 'wide'), may hold values from -0.0625 to 0.0625
- value_matrix: bfloat16 [4, 8192, 1024], P('segment', None, 'wide'), may hold values from -0.0625 to 0.0625
- output_matrix: bfloat16 [4, 8192, 8192], P('segment', None, 'wide'), may hold values from -0.0625 to 0.0625
- adapter_down_maps: bfloat16 [4, 8, 8192, 128], P('segment', 'wide'), may hold values from -0.0625 to 0.0625
- adapter_up_query: bfloat16 [4, 8, 64, 8192], P('segment', 'wide'), may hold values from -0.75 to 0.75
- adapter_up_value: bfloat16 [4, 8, 64, 1024], P('segment', 'wide'), may hold values from -0.75 to 0.75
- rotated_key_cache: bfloat16 [4, 2, 16, 384, 1024], P('segment', None, 'wide'), may hold values from -480 to 480
- cached_values: bfloat16 [4, 2, 16, 384, 1024], P('segment', None, 'wide'), may hold values from -6 to 6
Outputs:
- layer_out: bfloat16 [4, 2, 16, 8192], P('segment', None, 'wide')
Inputs may be any that keep to these rules, and one draw needn't show every extreme that they name: `row_adapter_index`: in each micro-batch no adapter is named by more than 4 rows.
All inputs are finite; a program needn't handle non-finite values.
Results may differ from a plain program's by a relative error of at most 0.038.
Values may be sent and summed in bfloat16 or wider, within the bound.
No kernel may reach another device: no remote copies, remote signals or barrier semaphores. Data moves between devices by JAX's collectives and lax.ppermute only.
A program may use at most 128 MiB of HBM per device.

v0:
```python
import functools

import jax
import jax.numpy as jnp
from jax import lax
from jax.experimental import pallas as pl
from jax.experimental.pallas import tpu as pltpu
from jax.sharding import PartitionSpec as P

HEADS = 64
KVH = 8
HD = 128
ADAPTER_RANK = 64
CAP = 4


adapter_scale = 0.5
rope_base = 500000.0
epsilon = 1e-05

GROUP = HEADS // KVH
MIB = 1 << 20
VMEM = pl.BlockSpec(memory_space=pltpu.VMEM)
SMEM = pl.BlockSpec(memory_space=pltpu.SMEM)


def swapped(value, bits):
    count = lax.axis_size("wide")
    return lax.ppermute(value, "wide", [(i, i ^ bits) for i in range(count)])


def gathered(value):
    count = lax.axis_size("wide")
    found = [None] * count
    found[0] = value
    found[1] = swapped(value, 1)
    for far in range(2, count, 2):
        found[far] = swapped(value, far)
    for far in range(2, count, 2):
        found[far + 1] = swapped(found[far], 1)
    return found


def exchanged(blocks):
    found = []
    for k, block in enumerate(blocks):
        found.append(swapped(block, 2 * k) if k else block)
    return [part for far in found for part in (far, swapped(far, 1))]


def own_half(j, block):
    half = block.shape[0] // 2
    return block[(j % 2) * half : (j % 2 + 1) * half, :]


def resident(weight):
    return pltpu.with_memory_space_constraint(weight, pltpu.VMEM)


def call(body, out_shape, operands, scratch=(), limit=8, kept=(), name=None):
    outs = list(out_shape)
    found = pl.pallas_call(
        body,
        out_shape=outs,
        in_specs=[spec for _, spec in operands] + [VMEM] * len(kept),
        out_specs=[VMEM] * len(outs),
        scratch_shapes=list(scratch),
        compiler_params=pltpu.CompilerParams(vmem_limit_bytes=limit * MIB),
        name=name,
    )(*[array for array, _ in operands], *[resident(array) for array in kept])
    return [*found, *kept]


def dot(left, right):
    return jnp.dot(left, right, preferred_element_type=jnp.float32)


def matmul_into(store, source, weight, step):
    def one(i, carry):
        columns = pl.ds(pl.multiple_of(i * step, step), step)
        store(columns, dot(source[...], weight[:, columns]))
        return carry

    lax.fori_loop(0, weight.shape[1] // step, one, 0)


def by_part(owner, chunks, own_rows):
    count = len(chunks)
    parts = chunks[0].shape[0] // own_rows
    total = count * parts * own_rows
    stack = jnp.concatenate([chunk[...] for chunk in chunks], 0)
    out = lax.broadcasted_iota(jnp.int32, (total, total), 0)
    src = lax.broadcasted_iota(jnp.int32, (total, total), 1)
    rows = own_rows
    part_out = out // (rows * count)
    device_out = (out // rows) % count
    part_src = (src // rows) % parts
    device_src = (src // (rows * parts)) ^ owner
    hit = (part_out == part_src) & (device_out == device_src) & (out % rows == src % rows)
    return dot(jnp.where(hit, 1.0, 0.0).astype(jnp.bfloat16), stack)


def adapter_part(owner, ident, normed, down, up_query, up_value, outs, capacity):
    rows = normed.shape[0]
    low = dot(normed[...], down[0]).astype(jnp.bfloat16)
    place = lax.broadcasted_iota(jnp.int32, (rows, rows), 0)
    other = lax.broadcasted_iota(jnp.int32, (rows, rows), 1)
    mine = jnp.where(ident[:, :1] == owner.astype(jnp.float32), 1.0, 0.0)
    flat = jnp.where(place == other, mine, 0.0).astype(jnp.bfloat16)
    before = jnp.where(place < other, mine, 0.0).astype(jnp.bfloat16)
    ones = jnp.ones((capacity, rows), jnp.bfloat16)
    member = dot(ones, flat)
    rank = dot(ones, before)
    slot = lax.broadcasted_iota(jnp.int32, (capacity, rows), 0).astype(jnp.float32)
    chosen = jnp.where((member > 0.5) & (rank == slot), 1.0, 0.0).astype(jnp.bfloat16)
    picked = dot(chosen, low).astype(jnp.bfloat16)
    count = 2 * len(outs)
    query_cols = up_query.shape[2] // count
    value_cols = up_value.shape[2] // count
    for j in range(count):
        out = outs[j // 2]
        slots = slice((j % 2) * capacity, (j % 2 + 1) * capacity)
        columns = pl.ds(pl.multiple_of((owner ^ j) * query_cols, query_cols), query_cols)
        for_query = dot(picked[:, :ADAPTER_RANK], up_query[0, :, columns]) * adapter_scale
        out[slots, :query_cols] = for_query.astype(jnp.bfloat16)
        columns = pl.ds(pl.multiple_of((owner ^ j) * value_cols, value_cols), value_cols)
        for_value = dot(picked[:, ADAPTER_RANK:], up_value[0, :, columns]) * adapter_scale
        out[slots, query_cols:] = for_value.astype(jnp.bfloat16)


def enter_kernel(count, own_rows, capacity, owner_ref, *refs):
    chunks, rest = refs[:count], refs[count:]
    gain, down, up_query, up_value, normed, held, ident, *correction, spread = rest
    owner = owner_ref[0]
    rows = count * own_rows
    part = gain.shape[1] // count
    spread[...] = by_part(owner, chunks, own_rows)
    ident[...] = spread[:rows, part:]
    squares = jnp.zeros((rows, 1), jnp.float32)
    for i in range(count):
        block = spread[i * rows : (i + 1) * rows, :part]
        squares += jnp.sum(block * block, 1, keepdims=True)
    scale = lax.rsqrt(squares / gain.shape[1] + epsilon)
    for i in range(count):
        block = spread[i * rows : (i + 1) * rows, :part]
        columns = slice(i * part, (i + 1) * part)
        weight = gain[:, columns].astype(jnp.float32)
        normed[:, columns] = (block * scale * weight).astype(jnp.bfloat16)
    own = pl.ds(pl.multiple_of(owner * rows, rows), rows)
    held[...] = spread[own, :part].astype(jnp.bfloat16)
    adapter_part(owner, ident, normed, down, up_query, up_value, correction, capacity)


def norm_kernel(count, capacity, owner_ref, *refs):
    chunks, rest = refs[:count], refs[count:]
    ident, gain, down, up_query, up_value, normed, *correction = rest
    owner = owner_ref[0]
    rows, part = chunks[0].shape
    squares = jnp.zeros((rows, 1), jnp.float32)
    for chunk in chunks:
        block = chunk[...].astype(jnp.float32)
        squares += jnp.sum(block * block, 1, keepdims=True)
    scale = lax.rsqrt(squares / gain.shape[1] + epsilon)
    for k, chunk in enumerate(chunks):
        columns = pl.ds(pl.multiple_of((owner ^ k) * part, part), part)
        weight = gain[:, columns].astype(jnp.float32)
        normed[:, columns] = (chunk[...].astype(jnp.float32) * scale * weight).astype(jnp.bfloat16)
    adapter_part(owner, ident, normed, down, up_query, up_value, correction, capacity)


def project_kernel(normed, query, key, value, out):
    wide, narrow = query.shape[1], key.shape[1]

    def store(columns, product):
        out[:, columns] = product

    matmul_into(store, normed, query, 256)
    out[:, wide : wide + narrow] = dot(normed[...], key[...])
    out[:, wide + narrow :] = dot(normed[...], value[...])


def correct_kernel(count, capacity, query_cols, key_cols, owner_ref, base, ident, *refs):
    received, outs = refs[:count], refs[count:]
    owner = owner_ref[0]
    rows = base.shape[0]
    own_rows = rows // count
    slots = count * capacity
    place = lax.broadcasted_iota(jnp.int32, (rows, rows), 0)
    other = lax.broadcasted_iota(jnp.int32, (rows, rows), 1)
    own = ident[:, :1]
    flat = jnp.where(place == other, own, 0.0).astype(jnp.bfloat16)
    line = dot(jnp.ones((rows, rows), jnp.bfloat16), flat)
    rank = jnp.sum(jnp.where((own == line) & (other < place), 1.0, 0.0), 1, keepdims=True)
    slot = lax.broadcasted_iota(jnp.int32, (rows, slots), 1)
    source = ((slot // capacity) ^ owner).astype(jnp.float32)
    hit = (source == own) & ((slot % capacity).astype(jnp.float32) == rank)
    table = jnp.where(hit, 1.0, 0.0).astype(jnp.bfloat16)
    placed = dot(table, jnp.concatenate([own_half(j, ref) for j, ref in enumerate(received)], 0))
    whole = base[...]
    first = whole[:, :query_cols] + placed[:, :query_cols]
    middle = whole[:, query_cols : query_cols + key_cols]
    last = whole[:, query_cols + key_cols :] + placed[:, query_cols:]
    packed = jnp.concatenate([first, middle, last], 1).astype(jnp.bfloat16)
    by_destination(owner, packed, own_rows, outs)


def by_destination(owner, packed, own_rows, outs):
    rows = packed.shape[0]
    place = lax.broadcasted_iota(jnp.int32, (rows, rows), 0)
    other = lax.broadcasted_iota(jnp.int32, (rows, rows), 1)
    hit = (((place // own_rows) ^ owner) == other // own_rows) & (
        place % own_rows == other % own_rows
    )
    order = jnp.where(hit, 1.0, 0.0).astype(jnp.bfloat16)
    sorted_rows = dot(order, packed).astype(jnp.bfloat16)
    for k, out in enumerate(outs):
        out[...] = sorted_rows[k * 2 * own_rows : (k + 1) * 2 * own_rows, :]


def attend_kernel(count, owner_ref, lengths, *refs):
    arrived, (cosine, sine, keys, values, out) = refs[:count], refs[count:]
    owner = owner_ref[0]
    own_rows, span = keys.shape[:2]
    rows = GROUP * own_rows
    cos, sin = cosine[...], sine[...]
    row_of = lax.broadcasted_iota(jnp.int32, (rows, span), 0) % own_rows
    position = lax.broadcasted_iota(jnp.int32, (rows, span), 1)
    limit = jnp.zeros((rows, span), jnp.int32)
    for r in range(own_rows):
        limit = jnp.where(row_of == r, lengths[r], limit)
    valid = position < limit
    score_scale = HD ** (-0.5)

    def turned(vectors):
        return vectors * cos + pltpu.roll(vectors, HD // 2, 1) * sin

    def rounded(vectors):
        return vectors.astype(jnp.bfloat16).astype(jnp.float32)

    for j, ref in enumerate(arrived):
        packed = own_half(j, ref).astype(jnp.float32)
        query = jnp.concatenate([packed[:, i * HD : (i + 1) * HD] for i in range(GROUP)], 0)
        new_key = packed[:, GROUP * HD : (GROUP + 1) * HD]
        new_value = packed[:, (GROUP + 1) * HD :]
        new_key = jnp.concatenate([new_key] * GROUP, 0)
        new_value = jnp.concatenate([new_value] * GROUP, 0)
        query = turned(query).astype(jnp.bfloat16)
        new_key = rounded(turned(new_key))
        lanes = pl.ds(pl.multiple_of((owner ^ j) * HD, HD), HD)
        scores = jnp.zeros((rows, span), jnp.float32)
        for r in range(own_rows):
            one = lax.dot_general(
                query,
                keys[r, :, lanes],
                (((1,), (1,)), ((), ())),
                preferred_element_type=jnp.float32,
            )
            scores = jnp.where(row_of == r, one, scores)
        scores = jnp.where(valid, scores * score_scale, -1e30)
        own = jnp.sum(query.astype(jnp.float32) * new_key, 1, keepdims=True) * score_scale
        top = jnp.maximum(jnp.max(scores, 1, keepdims=True), own)
        past = jnp.where(valid, jnp.exp(scores - top), 0.0)
        own = jnp.exp(own - top)
        total = jnp.sum(past, 1, keepdims=True) + own
        past = (past / total).astype(jnp.bfloat16)
        mixed = rounded(own / total) * new_value
        for r in range(own_rows):
            weights = jnp.where(row_of == r, past, jnp.zeros_like(past))
            mixed += dot(weights, values[r, :, lanes])
        out[:, lanes] = mixed.astype(jnp.bfloat16)


def leave_kernel(count, own_rows, tick, owner_ref, segment_ref, *refs):
    chunks, (held, result, matrix, out, kept, *outs, spread, rows_ref) = refs[:count], refs[count:]
    rows = count * own_rows
    spread[...] = by_part(owner_ref[0], chunks, own_rows).astype(jnp.bfloat16)
    for g in range(KVH):
        for j in range(GROUP):
            head = g * GROUP + j
            rows_ref[:, head * HD : (head + 1) * HD] = spread[
                j * rows : (j + 1) * rows, g * HD : (g + 1) * HD
            ]

    def store(columns, product):
        out[:, columns] = (held[:, columns].astype(jnp.float32) + product).astype(jnp.bfloat16)

    matmul_into(store, rows_ref, matrix, 256)
    kept[...] = jnp.where(segment_ref[0] == tick, out[...], result[...])
    if outs:
        by_destination(owner_ref[0], kept[...], own_rows, outs)


def join_kernel(count, owner_ref, *refs):
    blocks, out = refs[:count], refs[count]
    for j, block in enumerate(blocks):
        half = own_half(j, block)
        width = half.shape[1]
        out[:, pl.ds(pl.multiple_of((owner_ref[0] ^ j) * width, width), width)] = half


def on_device_by_head(
    entering_hidden,
    row_adapter_index,
    lengths,
    input_norm_gain,
    query_matrix,
    key_matrix,
    value_matrix,
    output_matrix,
    adapter_down_maps,
    adapter_up_query,
    adapter_up_value,
    rotated_key_cache,
    cached_values,
):
    segments = lax.axis_size("segment")
    segment = lax.axis_index("segment")
    count = lax.axis_size("wide")
    owner = lax.axis_index("wide")
    owner_ref = owner.astype(jnp.int32).reshape(1)
    segment_ref = segment.astype(jnp.int32).reshape(1)
    micro, local_rows, width = entering_hidden.shape
    own_rows = micro * local_rows
    rows = own_rows * count
    capacity = CAP * micro
    part = width // count
    query_cols, key_cols = query_matrix.shape[2], key_matrix.shape[2]
    packed_cols = query_cols + 2 * key_cols
    span = rotated_key_cache.shape[3]

    query_weight = query_matrix[0]
    key_weight = key_matrix[0]
    value_weight = value_matrix[0]
    output_weight = output_matrix[0]
    down = adapter_down_maps[0]
    up_query = adapter_up_query[0]
    up_value = adapter_up_value[0]
    keys = rotated_key_cache[0].reshape(own_rows, span, -1)
    values = cached_values[0].reshape(own_rows, span, -1)
    gain = input_norm_gain

    positions = lengths.reshape(-1)
    half = HD // 2
    inverse = rope_base ** (-jnp.arange(half, dtype=jnp.float32) / half)
    angles = positions.astype(jnp.float32)[:, None] * inverse[None, :]
    cosine = jnp.tile(jnp.concatenate([jnp.cos(angles)] * 2, 1), (GROUP, 1))
    sine = jnp.tile(jnp.concatenate([-jnp.sin(angles), jnp.sin(angles)], 1), (GROUP, 1))

    def blocks_of(slots, columns):
        return [jax.ShapeDtypeStruct((2 * slots, columns), jnp.bfloat16)] * (count // 2)

    normed_shape = jax.ShapeDtypeStruct((rows, width), jnp.bfloat16)
    held_shape = jax.ShapeDtypeStruct((rows, part), jnp.bfloat16)
    ident_shape = jax.ShapeDtypeStruct((rows, HD), jnp.float32)
    correction_shapes = blocks_of(capacity, query_cols + key_cols)

    own = entering_hidden.reshape(own_rows, count, part).transpose(1, 0, 2)
    names = row_adapter_index.reshape(1, own_rows, 1).astype(jnp.bfloat16)
    names = jnp.broadcast_to(names, (count, own_rows, HD))
    entering = jnp.concatenate([own, names], 2).reshape(count * own_rows, part + HD)

    adapters = [down, up_query, up_value]
    projections = [query_weight, key_weight, value_weight]
    caches = [keys, values]
    outputs = [output_weight]
    held = ident = None
    result = jnp.zeros((rows, part), jnp.bfloat16)
    blocks = []
    for tick in range(segments):
        if tick == 0:
            chunks = gathered(entering)
            normed, held, ident, *found = call(
                functools.partial(enter_kernel, count, own_rows, capacity),
                [normed_shape, held_shape, ident_shape] + correction_shapes,
                [(owner_ref, SMEM)] + [(c, VMEM) for c in chunks] + [(gain, VMEM)],
                [pltpu.VMEM((count * rows, part + HD), jnp.float32)],
                kept=adapters,
                name="enter",
            )
        else:
            held = lax.ppermute(
                held, "segment", [(s, (s + 1) % segments) for s in range(segments)]
            )
            chunks = gathered(held)
            normed, *found = call(
                functools.partial(norm_kernel, count, capacity),
                [normed_shape] + correction_shapes,
                [(owner_ref, SMEM)] + [(c, VMEM) for c in chunks] + [(ident, VMEM), (gain, VMEM)],
                kept=adapters,
                name="norm",
            )
        correction, adapters = found[: count // 2], found[count // 2 :]
        received = exchanged(correction)
        base, *projections = call(
            project_kernel,
            [jax.ShapeDtypeStruct((rows, packed_cols), jnp.float32)],
            [(normed, VMEM)],
            kept=projections,
            name="project",
        )
        packed = call(
            functools.partial(correct_kernel, count, capacity, query_cols, key_cols),
            blocks_of(own_rows, packed_cols),
            [(owner_ref, SMEM), (base, VMEM), (ident, VMEM)] + [(r, VMEM) for r in received],
            name="correct",
        )
        arrived = exchanged(packed)
        attended, *caches = call(
            functools.partial(attend_kernel, count),
            [jax.ShapeDtypeStruct((GROUP * own_rows, KVH * HD), jnp.bfloat16)],
            [(owner_ref, SMEM), (positions, SMEM)] + [(a, VMEM) for a in arrived]
            + [(cosine, VMEM), (sine, VMEM)],
            kept=caches,
            name="attend",
        )
        chunks = gathered(attended)
        last = tick == segments - 1
        held, result, *found = call(
            functools.partial(leave_kernel, count, own_rows, tick),
            [held_shape, held_shape] + (blocks_of(own_rows, part) if last else []),
            [(owner_ref, SMEM), (segment_ref, SMEM)] + [(c, VMEM) for c in chunks]
            + [(held, VMEM), (result, VMEM)],
            [
                pltpu.VMEM((GROUP * rows, KVH * HD), jnp.bfloat16),
                pltpu.VMEM((rows, width), jnp.bfloat16),
            ],
            kept=outputs,
            name="leave",
        )
        blocks, outputs = found[:-1], found[-1:]
    (joined,) = call(
        functools.partial(join_kernel, count),
        [jax.ShapeDtypeStruct((own_rows, width), jnp.bfloat16)],
        [(owner_ref, SMEM)] + [(b, VMEM) for b in exchanged(blocks)],
        name="join",
    )
    return joined.reshape(1, micro, local_rows, width)


def passed_along(value, axis, steps):
    count = lax.axis_size(axis)
    leading, last = (max(0, -steps), min(count, count - steps))
    return lax.ppermute(value, axis, [(source, source + steps) for source in range(leading, last)])


def rotary(vectors, positions):
    half = vectors.shape[-1] // 2
    inverse = rope_base ** (-jnp.arange(half, dtype=jnp.float32) / half)
    angles = positions.astype(jnp.float32)[:, None] * inverse[None, :]
    cosine = jnp.cos(angles)[:, None, :]
    sine = jnp.sin(angles)[:, None, :]
    front = vectors[..., :half]
    back = vectors[..., half:]
    return jnp.concatenate([front * cosine - back * sine, back * cosine + front * sine], -1)


def attend(query_vector, new_key, fresh_value, positions, key_block, value_block):
    rows = query_vector.shape[0]
    group = HEADS // KVH
    rotated_rows = rotary(
        query_vector.astype(jnp.float32).reshape(rows, HEADS, HD), positions
    ).astype(jnp.bfloat16)
    rotated_rows = rotated_rows.reshape(rows, KVH, group, HD)
    self_key = rotary(new_key.astype(jnp.float32).reshape(rows, KVH, HD), positions).astype(
        jnp.bfloat16
    )
    keys_past = key_block.reshape(rows, -1, KVH, HD)
    values_past = value_block.reshape(rows, -1, KVH, HD)
    score_scale = HD ** (-0.5)
    past = (
        jnp.einsum("bkgd,bpkd->bkgp", rotated_rows, keys_past, preferred_element_type=jnp.float32)
        * score_scale
    )
    self_scores = (
        jnp.einsum("rice,rie->ric", rotated_rows, self_key, preferred_element_type=jnp.float32)
        * score_scale
    )
    valid = jnp.arange(keys_past.shape[1])[None, :] < positions[:, None]
    past = jnp.where(valid[:, None, None, :], past, -1e30)
    top = jnp.maximum(jnp.max(past, -1), self_scores)
    past_exp = jnp.where(valid[:, None, None, :], jnp.exp(past - top[..., None]), 0.0)
    own_exp = jnp.exp(self_scores - top)
    total = jnp.sum(past_exp, -1) + own_exp
    past_weights = (past_exp / total[..., None]).astype(jnp.bfloat16)
    own_weights = (own_exp / total).astype(jnp.bfloat16)
    mixed = jnp.einsum(
        "bkgp,bpkd->bkgd", past_weights, values_past, preferred_element_type=jnp.float32
    )
    mixed = (
        mixed
        + own_weights.astype(jnp.float32)[..., None]
        * fresh_value.reshape(rows, KVH, HD).astype(jnp.float32)[:, :, None, :]
    )
    return mixed.reshape(rows, HEADS * HD).astype(jnp.bfloat16)


def on_device(
    entering_hidden,
    row_adapter_index,
    lengths,
    input_norm_gain,
    query_matrix,
    key_matrix,
    value_matrix,
    output_matrix,
    adapter_down_maps,
    adapter_up_query,
    adapter_up_value,
    rotated_key_cache,
    cached_values,
):
    segments = lax.axis_size("segment")
    segment = lax.axis_index("segment")
    devices = lax.axis_size("wide")
    owner = lax.axis_index("wide")
    small_batch, local_rows, width = entering_hidden.shape
    listed = lax.all_gather(row_adapter_index, "wide", axis=1, tiled=True)[:, :, 0]
    groups = small_batch // small_batch
    capacity = CAP * small_batch
    kept_entries = adapter_down_maps.shape[1]
    adapters = kept_entries * devices
    mine = owner * kept_entries + jnp.arange(kept_entries)
    gain = input_norm_gain[0].astype(jnp.float32)
    query_cols = query_matrix.shape[2]
    key_cols = key_matrix.shape[2]
    passed = jnp.zeros((small_batch * local_rows, width), jnp.bfloat16)
    results = jnp.zeros((small_batch, local_rows, width), jnp.bfloat16)
    ticks = groups + segments - 1
    for tick in range(ticks):
        if tick < groups:
            fresh = entering_hidden.reshape(small_batch * local_rows, width)
        else:
            fresh = jnp.zeros_like(passed)
        rows = jnp.where(segment == 0, fresh, passed)
        index = tick - segment
        live = (index >= 0) & (index < groups)
        index = jnp.clip(index, 0, groups - 1)
        block_rows = rows.shape[0]
        idents = listed
        idents = idents.reshape(small_batch, devices, local_rows).transpose(1, 0, 2).reshape(-1)
        positions = lengths.reshape(-1)
        key_block = rotated_key_cache[0]
        key_block = key_block.reshape(block_rows, key_block.shape[2], key_block.shape[3])
        value_block = cached_values[0]
        value_block = value_block.reshape(block_rows, value_block.shape[2], value_block.shape[3])
        values = rows.astype(jnp.float32)
        normalized_rows = (
            values * lax.rsqrt(jnp.mean(values * values, 1, keepdims=True) + epsilon) * gain
        ).astype(jnp.bfloat16)
        gathered = lax.all_gather(normalized_rows, "wide", axis=0, tiled=True)
        total_rows = gathered.shape[0]
        matches = (idents[None, :] == mine[:, None]).astype(jnp.int32)
        ranks = jnp.cumsum(matches, 1) - 1
        chosen = (matches[:, None, :] == 1) & (
            ranks[:, None, :] == jnp.arange(capacity)[None, :, None]
        )
        chosen = chosen.reshape(kept_entries * capacity, total_rows)
        selected_rows = jnp.dot(
            chosen.astype(jnp.bfloat16), gathered, preferred_element_type=jnp.float32
        ).astype(jnp.bfloat16)
        selected_rows = selected_rows.reshape(kept_entries, capacity, width)
        reduced = jnp.einsum(
            "bpy,byf->bpf", selected_rows, adapter_down_maps[0], preferred_element_type=jnp.float32
        ).astype(jnp.bfloat16)
        member = (idents[:, None] == jnp.arange(adapters)[None, :]).astype(jnp.int32)
        order = jnp.sum(jnp.cumsum(member, 0) * member, 1) - 1
        slot = idents * capacity + order
        slot_table = slot[:, None] == jnp.arange(adapters * capacity)[None, :]
        query_slots = jnp.einsum(
            "acr,are->ace",
            reduced[..., :ADAPTER_RANK],
            adapter_up_query[0],
            preferred_element_type=jnp.float32,
        )
        value_slots = jnp.einsum(
            "acr,are->ace",
            reduced[..., ADAPTER_RANK:],
            adapter_up_value[0],
            preferred_element_type=jnp.float32,
        )
        joined = jnp.concatenate(
            [
                query_slots.reshape(kept_entries * capacity, devices, -1),
                value_slots.reshape(kept_entries * capacity, devices, -1),
            ],
            2,
        )
        received = lax.all_to_all(joined, "wide", split_axis=1, concat_axis=0, tiled=True)
        received = received.reshape(adapters * capacity, -1)
        placed = jnp.dot(slot_table.astype(jnp.float32), received, precision=lax.Precision.HIGHEST)
        query_adjustment = placed[:, :query_cols]
        value_adjustment = placed[:, query_cols:]
        query_vector = (
            jnp.dot(gathered, query_matrix[0], preferred_element_type=jnp.float32)
            + adapter_scale * query_adjustment
        ).astype(jnp.bfloat16)
        new_key = jnp.dot(gathered, key_matrix[0], preferred_element_type=jnp.float32).astype(
            jnp.bfloat16
        )
        fresh_value = (
            jnp.dot(gathered, value_matrix[0], preferred_element_type=jnp.float32)
            + adapter_scale * value_adjustment
        ).astype(jnp.bfloat16)
        packed = jnp.concatenate([query_vector, new_key, fresh_value], 1)
        arrived = lax.all_to_all(packed, "wide", split_axis=0, concat_axis=1, tiled=True).reshape(
            block_rows, devices, -1
        )
        query_rows_local = arrived[:, :, :query_cols].reshape(block_rows, -1)
        key_rows_local = arrived[:, :, query_cols : query_cols + key_cols].reshape(block_rows, -1)
        value_rows_local = arrived[:, :, query_cols + key_cols :].reshape(block_rows, -1)
        attended = attend(
            query_rows_local, key_rows_local, value_rows_local, positions, key_block, value_block
        )
        columns = jnp.dot(
            lax.all_gather(attended, "wide", axis=0, tiled=True),
            output_matrix[0],
            preferred_element_type=jnp.float32,
        )
        returned = lax.all_to_all(columns, "wide", split_axis=0, concat_axis=1, tiled=True)
        outcome = (values + returned).astype(jnp.bfloat16)
        updated = outcome.reshape(small_batch, local_rows, width)
        results = jnp.where(live, updated, results)
        if tick + 1 < ticks:
            passed = passed_along(outcome, "segment", 1)
    return results[None]


def solution(mesh):
    placed = (
        P(None, "wide", None),
        P(None, "wide", None),
        P(None, "wide"),
        P("segment", None),
        P("segment", None, "wide"),
        P("segment", None, "wide"),
        P("segment", None, "wide"),
        P("segment", None, "wide"),
        P("segment", "wide", None, None),
        P("segment", "wide", None, None),
        P("segment", "wide", None, None),
        P("segment", None, "wide", None, None),
        P("segment", None, "wide", None, None),
    )
    by_head = mesh.shape["wide"] == KVH
    return jax.shard_map(
        on_device_by_head if by_head else on_device,
        mesh=mesh,
        in_specs=placed,
        out_specs=P("segment", None, "wide", None),
        check_vma=False,
    )
```

profile of v0, /device:TPU:7, one launch (start us, length us, event | category | flops | bytes accessed | tf_op | source)
XLA Modules:
  0.0 269.0 jit_solution(2731012969827025490)
XLA Ops:
  3.2 2.3 collective-permute-start.3
  7.9 4.1 %collective-permute-start.4 = (bf16[32,1152]{1,0:T(8,128)(2,1)S(1)}, bf16[32,1152]{1,0:T(8,128)(2,1)S(1)}, u32[]{:S(2)}, u32[]{:S(2)}) collective-permute-start(bf16[32,1152]{1,0:T(8,128)(2,1)S(1)} %collective-permute-done.3.refs_4_), channel_id=1, source_target_pairs={{0,1},{1,0},{2,3},{3,2},{4,5},{5,4},{6,7},{7,6},{8,9},{9,8},{10,11... | collective-permute-start | bytes 221192 | tf_op jit(solution)/shard_map/ppermute | solution.py:29
  14.0 1.6 copy-done.7
  20.7 1.8 collective-permute-start.10
  24.5 1.5 collective-permute-start.11
  27.1 1.8 collective-permute-start.13
  29.0 5.8 %copy-done = bf16[1,8192,1024]{2,1,0:T(8,128)(2,1)S(1)} copy-done((bf16[1,8192,1024]{2,1,0:T(8,128)(2,1)S(1)}, bf16[1,8192,1024]{2,1,0:T(8,128)(2,1)}, u32[]{:S(2)}) %copy-start) | copy-done | bytes 16777240
  34.8 1.6 copy-done.10
  36.4 1.6 copy-done.13
  39.0 4.1 %project.4.base = f32[32,1280]{1,0:T(8,128)S(1)} custom-call(bf16[32,8192]{1,0:T(8,128)(2,1)S(1)} %copy-done.23, bf16[8192,1024]{1,0:T(8,128)(2,1)S(1)} %bitcast.16, bf16[8192,128]{1,0:T(8,128)(2,1)S(1)} %bitcast.40, bf16[8192,128]{1,0:T(8,128)(2,1)S(1)} %bitcast.44), custom_call_target="tpu_custom_call" | custom-call | tf_op jit(solution)/shard_map/project/pallas_call | solution.py:62
  44.6 2.0 collective-permute-start.17
  46.6 1.5 collective-permute-start.19
  51.0 1.7 collective-permute-start.20
  53.6 4.7 %attend.4.refs_0_ = bf16[32,1024]{1,0:T(8,128)(2,1)S(1)} custom-call(s32[1]{0:T(128)} %bitcast.owner_ref, s32[4]{0:T(128)S(1)} %reshape.48.lengths, bf16[8,1280]{1,0:T(8,128)(2,1)S(1)} %get-tuple-element.59.refs_0_, bf16[8,1280]{1,0:T(8,128)(2,1)S(1)} %collective-permute-done.14.refs_1_, bf16[8,1280]{1,0:T(8,128)(2,1)S(1)} %collective-permute-done.15.refs_2_, ...), custom_call_target="tpu_custom_call" | custom-call | tf_op jit(solution)/shard_map/attend/pallas_call | solution.py:62
  58.4 2.3 collective-permute-start.24
  64.7 1.8 collective-permute-start.25
  69.1 5.8 %copy-done.2 = bf16[1,8192,1024]{2,1,0:T(8,128)(2,1)S(1)} copy-done((bf16[1,8192,1024]{2,1,0:T(8,128)(2,1)S(1)}, bf16[1,8192,1024]{2,1,0:T(8,128)(2,1)}, u32[]{:S(2)}) %copy-start.2) | copy-done | bytes 16777240
  76.6 5.0 %leave.4 = (bf16[32,1024]{1,0:T(8,128)(2,1)S(1)}, bf16[32,1024]{1,0:T(8,128)(2,1)S(1)}) custom-call(s32[1]{0:T(128)} %bitcast.owner_ref, s32[1]{0:T(128)} %bitcast.1.segment_ref, bf16[32,1024]{1,0:T(8,128)(2,1)S(1)} %attend.4.refs_0_, bf16[32,1024]{1,0:T(8,128)(2,1)} %collective-permute-done.21.refs_1_, bf16[32,1024]{1,0:T(8,128)(2,1)S(1)} %copy-done.27, ...), custom_call_target="tpu_custom_call" | custom-call | tf_op jit(solution)/shard_map/leave/pallas_call | solution.py:62
  82.1 2.9 %collective-permute-done.28.refs_0_.refs_8_ = bf16[32,1024]{1,0:T(8,128)(2,1)S(1)} collective-permute-done((bf16[32,1024]{1,0:T(8,128)(2,1)S(1)}, bf16[32,1024]{1,0:T(8,128)(2,1)S(1)}, u32[]{:S(2)}, u32[]{:S(2)}) %collective-permute-start.28) | collective-permute-done | bytes 65568 | tf_op jit(solution)/shard_map/ppermute | solution.py:381
  85.7 2.5 collective-permute-start.32
  88.5 2.3 collective-permute-start.29
  91.1 3.0 %collective-permute-start.33 = (bf16[32,1024]{1,0:T(8,128)(2,1)S(1)}, bf16[32,1024]{1,0:T(8,128)(2,1)S(1)}, u32[]{:S(2)}, u32[]{:S(2)}) collective-permute-start(bf16[32,1024]{1,0:T(8,128)(2,1)S(1)} %collective-permute-done.32.refs_4_), channel_id=1, source_target_pairs={{0,1},{1,0},{2,3},{3,2},{4,5},{5,4},{6,7},{7,6},{8,9},{9,8},{10,11... | collective-permute-start | bytes 196616 | tf_op jit(solution)/shard_map/ppermute | solution.py:29
  94.1 1.7 collective-permute-start.35
  98.0 1.7 collective-permute-start.39
  99.7 1.8 collective-permute-start.41
  104.5 1.7 collective-permute-start.42
  106.2 5.8 %copy-done.1 = bf16[1,8192,1024]{2,1,0:T(8,128)(2,1)S(1)} copy-done((bf16[1,8192,1024]{2,1,0:T(8,128)(2,1)S(1)}, bf16[1,8192,1024]{2,1,0:T(8,128)(2,1)}, u32[]{:S(2)}) %copy-start.1) | copy-done | bytes 16777240
  112.0 4.1 %project.5.base = f32[32,1280]{1,0:T(8,128)S(1)} custom-call(bf16[32,8192]{1,0:T(8,128)(2,1)S(1)} %get-tuple-element.65.normed, bf16[8192,1024]{1,0:T(8,128)(2,1)S(1)} %bitcast.17, bf16[8192,128]{1,0:T(8,128)(2,1)S(1)} %bitcast.41, bf16[8192,128]{1,0:T(8,128)(2,1)S(1)} %bitcast.45), custom_call_target="tpu_custom_call" | custom-call | tf_op jit(solution)/shard_map/project/pallas_call | solution.py:62
  116.8 2.3 collective-permute-start.46
  121.7 1.8 collective-permute-done.48.refs_6_
  123.6 1.7 collective-permute-start.49
  126.1 4.7 %attend.5.refs_0_ = bf16[32,1024]{1,0:T(8,128)(2,1)S(1)} custom-call(s32[1]{0:T(128)} %bitcast.owner_ref, s32[4]{0:T(128)S(1)} %reshape.48.lengths, bf16[8,1280]{1,0:T(8,128)(2,1)S(1)} %get-tuple-element.70.refs_0_, bf16[8,1280]{1,0:T(8,128)(2,1)S(1)} %collective-permute-done.43.refs_1_, bf16[8,1280]{1,0:T(8,128)(2,1)S(1)} %collective-permute-done.44.refs_2_, ...), custom_call_target="tpu_custom_call" | custom-call | tf_op jit(solution)/shard_map/attend/pallas_call | solution.py:62
  130.9 1.5 collective-permute-start.53
  132.4 2.0 collective-permute-start.55
  136.4 3.5 %collective-permute-start.54 = (bf16[32,1024]{1,0:T(8,128)(2,1)S(1)}, bf16[32,1024]{1,0:T(8,128)(2,1)S(1)}, u32[]{:S(2)}, u32[]{:S(2)}) collective-permute-start(bf16[32,1024]{1,0:T(8,128)(2,1)S(1)} %collective-permute-done.53.refs_4_), channel_id=1, source_target_pairs={{0,1},{1,0},{2,3},{3,2},{4,5},{5,4},{6,7},{7,6},{8,9},{9,8},{10,11... | collective-permute-start | bytes 196616 | tf_op jit(solution)/shard_map/ppermute | solution.py:29
  141.2 3.8 %leave.5 = (bf16[32,1024]{1,0:T(8,128)(2,1)S(1)}, bf16[32,1024]{1,0:T(8,128)(2,1)S(1)}) custom-call(s32[1]{0:T(128)} %bitcast.owner_ref, s32[1]{0:T(128)} %bitcast.1.segment_ref, bf16[32,1024]{1,0:T(8,128)(2,1)S(1)} %attend.5.refs_0_, bf16[32,1024]{1,0:T(8,128)(2,1)S(1)} %collective-permute-done.50.refs_1_, ...), custom_call_target="tpu_custom_call" | custom-call | tf_op jit(solution)/shard_map/leave/pallas_call | solution.py:62
  146.5 2.4 collective-permute-done.57.refs_0_.refs_8_
  150.0 2.4 collective-permute-start.63
  152.5 1.8 collective-permute-start.58
  154.5 3.0 %collective-permute-start.62 = (bf16[32,1024]{1,0:T(8,128)(2,1)S(1)}, bf16[32,1024]{1,0:T(8,128)(2,1)S(1)}, u32[]{:S(2)}, u32[]{:S(2)}) collective-permute-start(bf16[32,1024]{1,0:T(8,128)(2,1)S(1)} %collective-permute-done.61.refs_4_), channel_id=1, source_target_pairs={{0,1},{1,0},{2,3},{3,2},{4,5},{5,4},{6,7},{7,6},{8,9},{9,8},{10,11... | collective-permute-start | bytes 196616 | tf_op jit(solution)/shard_map/ppermute | solution.py:29
  165.5 1.9 collective-permute-start.69
  167.4 1.9 collective-permute-start.71
  169.4 4.1 %project.6.base = f32[32,1280]{1,0:T(8,128)S(1)} custom-call(bf16[32,8192]{1,0:T(8,128)(2,1)S(1)} %get-tuple-element.76.normed, bf16[8192,1024]{1,0:T(8,128)(2,1)S(1)} %bitcast.20, bf16[8192,128]{1,0:T(8,128)(2,1)S(1)} %bitcast.42, bf16[8192,128]{1,0:T(8,128)(2,1)S(1)} %bitcast.46), custom_call_target="tpu_custom_call" | custom-call | tf_op jit(solution)/shard_map/project/pallas_call | solution.py:62
  174.2 1.6 collective-permute-start.75
  175.8 1.9 collective-permute-start.77
  180.3 1.7 collective-permute-start.78
  182.8 4.7 %attend.6.refs_0_ = bf16[32,1024]{1,0:T(8,128)(2,1)S(1)} custom-call(s32[1]{0:T(128)} %bitcast.owner_ref, s32[4]{0:T(128)S(1)} %reshape.48.lengths, bf16[8,1280]{1,0:T(8,128)(2,1)S(1)} %get-tuple-element.81.refs_0_, bf16[8,1280]{1,0:T(8,128)(2,1)S(1)} %collective-permute-done.72.refs_1_, bf16[8,1280]{1,0:T(8,128)(2,1)S(1)} %collective-permute-done.73.refs_2_, ...), custom_call_target="tpu_custom_call" | custom-call | tf_op jit(solution)/shard_map/attend/pallas_call | solution.py:62
  187.6 2.2 collective-permute-start.82
  193.2 2.6 collective-permute-start.83
  197.8 3.8 %leave.6 = (bf16[32,1024]{1,0:T(8,128)(2,1)S(1)}, bf16[32,1024]{1,0:T(8,128)(2,1)S(1)}) custom-call(s32[1]{0:T(128)} %bitcast.owner_ref, s32[1]{0:T(128)} %bitcast.1.segment_ref, bf16[32,1024]{1,0:T(8,128)(2,1)S(1)} %attend.6.refs_0_, bf16[32,1024]{1,0:T(8,128)(2,1)S(1)} %collective-permute-done.79.refs_1_, ...), custom_call_target="tpu_custom_call" | custom-call | tf_op jit(solution)/shard_map/leave/pallas_call | solution.py:62
  201.6 2.3 collective-permute-start.86
  203.9 2.2 collective-permute-done.86.refs_0_.refs_8_
  207.0 1.6 collective-permute-start.90
  209.7 1.7 collective-permute-start.87
  211.7 3.5 %collective-permute-start.91 = (bf16[32,1024]{1,0:T(8,128)(2,1)S(1)}, bf16[32,1024]{1,0:T(8,128)(2,1)S(1)}, u32[]{:S(2)}, u32[]{:S(2)}) collective-permute-start(bf16[32,1024]{1,0:T(8,128)(2,1)S(1)} %collective-permute-done.90.refs_4_), channel_id=1, source_target_pairs={{0,1},{1,0},{2,3},{3,2},{4,5},{5,4},{6,7},{7,6},{8,9},{9,8},{10,11... | collective-permute-start | bytes 196616 | tf_op jit(solution)/shard_map/ppermute | solution.py:29
  218.1 2.1 collective-permute-start.99
  220.2 1.5 collective-permute-start.97
  226.1 4.1 %project.7.base = f32[32,1280]{1,0:T(8,128)S(1)} custom-call(bf16[32,8192]{1,0:T(8,128)(2,1)S(1)} %get-tuple-element.87.normed, bf16[8192,1024]{1,0:T(8,128)(2,1)S(1)} %bitcast.21, bf16[8192,128]{1,0:T(8,128)(2,1)S(1)} %bitcast.43, bf16[8192,128]{1,0:T(8,128)(2,1)S(1)} %bitcast.47), custom_call_target="tpu_custom_call" | custom-call | tf_op jit(solution)/shard_map/project/pallas_call | solution.py:62
  232.6 1.9 collective-permute-start.106
  239.6 4.7 %attend.7.refs_0_ = bf16[32,1024]{1,0:T(8,128)(2,1)S(1)} custom-call(s32[1]{0:T(128)} %bitcast.owner_ref, s32[4]{0:T(128)S(1)} %reshape.48.lengths, bf16[8,1280]{1,0:T(8,128)(2,1)S(1)} %get-tuple-element.92.refs_0_, bf16[8,1280]{1,0:T(8,128)(2,1)S(1)} %collective-permute-done.101.refs_1_, bf16[8,1280]{1,0:T(8,128)(2,1)S(1)} %collective-permute-done.102.refs_2_, ...), custom_call_target="tpu_custom_call" | custom-call | tf_op jit(solution)/shard_map/attend/pallas_call | solution.py:62
  244.4 2.1 collective-permute-start.111
  250.0 2.6 collective-permute-start.112
  254.5 4.4 %leave.7 = (bf16[32,1024]{1,0:T(8,128)(2,1)}, bf16[32,1024]{1,0:T(8,128)(2,1)}, bf16[8,1024]{1,0:T(8,128)(2,1)S(1)}, bf16[8,1024]{1,0:T(8,128)(2,1)S(1)}, bf16[8...) custom-call(s32[1]{0:T(128)} %bitcast.owner_ref, s32[1]{0:T(128)} %bitcast.1.segment_ref, ...), custom_call_target="tpu_custom_call" | custom-call | tf_op jit(solution)/shard_map/leave/pallas_call | solution.py:62
  265.7 1.8 collective-permute-start.121
  (297 shorter events, 95.5 us)
Async XLA Ops:
  1.9 5.1 %collective-permute-start.1 = (bf16[32,1152]{1,0:T(8,128)(2,1)S(1)}, bf16[32,1152]{1,0:T(8,128)(2,1)S(1)}, u32[]{:S(2)}, u32[]{:S(2)}) collective-permute-start(bf16[32,1152]{1,0:T(8,128)(2,1)S(1)} %reshape.50.refs_0_), channel_id=1, source_target_pairs={{0,2},{1,3},{2,0},{3,1},{4,6},{5,7},{6,4},{7,5},{8,10},{9,11},{10,... | collective-permute-start | bytes 221192 | tf_op jit(solution)/shard_map/ppermute | solution.py:29
  5.6 6.4 %collective-permute-start.5 = (bf16[32,1152]{1,0:T(8,128)(2,1)S(1)}, bf16[32,1152]{1,0:T(8,128)(2,1)S(1)}, u32[]{:S(2)}, u32[]{:S(2)}) collective-permute-start(bf16[32,1152]{1,0:T(8,128)(2,1)S(1)} %reshape.50.refs_0_), channel_id=1, source_target_pairs={{0,6},{1,7},{2,4},{3,5},{4,2},{5,3},{6,0},{7,1},{8,14},{9,15},{10,... | collective-permute-start | bytes 221192 | tf_op jit(solution)/shard_map/ppermute | solution.py:29
  5.6 7.5 %collective-permute-start = (bf16[32,1152]{1,0:T(8,128)(2,1)S(1)}, bf16[32,1152]{1,0:T(8,128)(2,1)S(1)}, u32[]{:S(2)}, u32[]{:S(2)}) collective-permute-start(bf16[32,1152]{1,0:T(8,128)(2,1)S(1)} %reshape.50.refs_0_), channel_id=1, source_target_pairs={{0,1},{1,0},{2,3},{3,2},{4,5},{5,4},{6,7},{7,6},{8,9},{9,8},{10,11... | collective-permute-start | bytes 221192 | tf_op jit(solution)/shard_map/ppermute | solution.py:29
  7.0 6.0 %collective-permute-start.2 = (bf16[32,1152]{1,0:T(8,128)(2,1)S(1)}, bf16[32,1152]{1,0:T(8,128)(2,1)S(1)}, u32[]{:S(2)}, u32[]{:S(2)}) collective-permute-start(bf16[32,1152]{1,0:T(8,128)(2,1)S(1)} %collective-permute-done.1.refs_2_), channel_id=1, source_target_pairs={{0,1},{1,0},{2,3},{3,2},{4,5},{5,4},{6,7},{7,6},{8,9},{9,8},{10,11... | collective-permute-start | bytes 221192 | tf_op jit(solution)/shard_map/ppermute | solution.py:29
  7.9 5.2 %collective-permute-start.4 = (bf16[32,1152]{1,0:T(8,128)(2,1)S(1)}, bf16[32,1152]{1,0:T(8,128)(2,1)S(1)}, u32[]{:S(2)}, u32[]{:S(2)}) collective-permute-start(bf16[32,1152]{1,0:T(8,128)(2,1)S(1)} %collective-permute-done.3.refs_4_), channel_id=1, source_target_pairs={{0,1},{1,0},{2,3},{3,2},{4,5},{5,4},{6,7},{7,6},{8,9},{9,8},{10,11... | collective-permute-start | bytes 221192 | tf_op jit(solution)/shard_map/ppermute | solution.py:29
  23.6 5.3 %collective-permute-start.8 = (bf16[16,1152]{1,0:T(8,128)(2,1)S(1)}, bf16[16,1152]{1,0:T(8,128)(2,1)S(1)}, u32[]{:S(2)}, u32[]{:S(2)}) collective-permute-start(bf16[16,1152]{1,0:T(8,128)(2,1)S(1)} %get-tuple-element.56), channel_id=1, source_target_pairs={{0,2},{1,3},{2,0},{3,1},{4,6},{5,7},{6,4},{7,5},{8,10},{9,11},{10,... | collective-permute-start | bytes 110600 | tf_op jit(solution)/shard_map/ppermute | solution.py:29
  23.6 19.6 %collective-permute-start.7 = (bf16[16,1152]{1,0:T(8,128)(2,1)S(1)}, bf16[16,1152]{1,0:T(8,128)(2,1)S(1)}, u32[]{:S(2)}, u32[]{:S(2)}) collective-permute-start(bf16[16,1152]{1,0:T(8,128)(2,1)S(1)} %get-tuple-element.55.refs_0_), channel_id=1, source_target_pairs={{0,1},{1,0},{2,3},{3,2},{4,5},{5,4},{6,7},{7,6},{8,9},{9,8},{10,11... | collective-permute-start | bytes 110600 | tf_op jit(solution)/shard_map/ppermute | solution.py:29
  24.5 18.6 %collective-permute-start.11 = (bf16[16,1152]{1,0:T(8,128)(2,1)S(1)}, bf16[16,1152]{1,0:T(8,128)(2,1)S(1)}, u32[]{:S(2)}, u32[]{:S(2)}) collective-permute-start(bf16[16,1152]{1,0:T(8,128)(2,1)S(1)} %collective-permute-done.10.refs_4_), channel_id=1, source_target_pairs={{0,1},{1,0},{2,3},{3,2},{4,5},{5,4},{6,7},{7,6},{8,9},{9,8},{10,11... | collective-permute-start | bytes 110600 | tf_op jit(solution)/shard_map/ppermute | solution.py:29
  27.1 16.1 %collective-permute-start.13 = (bf16[16,1152]{1,0:T(8,128)(2,1)S(1)}, bf16[16,1152]{1,0:T(8,128)(2,1)S(1)}, u32[]{:S(2)}, u32[]{:S(2)}) collective-permute-start(bf16[16,1152]{1,0:T(8,128)(2,1)S(1)} %collective-permute-done.12.refs_6_), channel_id=1, source_target_pairs={{0,1},{1,0},{2,3},{3,2},{4,5},{5,4},{6,7},{7,6},{8,9},{9,8},{10,11... | collective-permute-start | bytes 110600 | tf_op jit(solution)/shard_map/ppermute | solution.py:29
  28.9 14.3 %collective-permute-start.9 = (bf16[16,1152]{1,0:T(8,128)(2,1)S(1)}, bf16[16,1152]{1,0:T(8,128)(2,1)}, u32[]{:S(2)}, u32[]{:S(2)}) collective-permute-start(bf16[16,1152]{1,0:T(8,128)(2,1)S(1)} %collective-permute-done.8.refs_2_), channel_id=1, source_target_pairs={{0,1},{1,0},{2,3},{3,2},{4,5},{5,4},{6,7},{7,6},{8,9},{9,8},{10,11... | collective-permute-start | bytes 110600 | tf_op jit(solution)/shard_map/ppermute | solution.py:29
  44.5 5.1 %collective-permute-start.15 = (bf16[8,1280]{1,0:T(8,128)(2,1)S(1)}, bf16[8,1280]{1,0:T(8,128)(2,1)S(1)}, u32[]{:S(2)}, u32[]{:S(2)}) collective-permute-start(bf16[8,1280]{1,0:T(8,128)(2,1)S(1)} %get-tuple-element.60), channel_id=1, source_target_pairs={{0,2},{1,3},{2,0},{3,1},{4,6},{5,7},{6,4},{7,5},{8,10},{9,11},{10,... | collective-permute-start | bytes 61448 | tf_op jit(solution)/shard_map/ppermute | solution.py:29
  44.6 5.1 %collective-permute-start.17 = (bf16[8,1280]{1,0:T(8,128)(2,1)S(1)}, bf16[8,1280]{1,0:T(8,128)(2,1)S(1)}, u32[]{:S(2)}, u32[]{:S(2)}) collective-permute-start(bf16[8,1280]{1,0:T(8,128)(2,1)S(1)} %get-tuple-element.61), channel_id=1, source_target_pairs={{0,4},{1,5},{2,6},{3,7},{4,0},{5,1},{6,2},{7,3},{8,12},{9,13},{10,... | collective-permute-start | bytes 61448 | tf_op jit(solution)/shard_map/ppermute | solution.py:29
  58.3 4.8 %collective-permute-start.22 = (bf16[32,1024]{1,0:T(8,128)(2,1)S(1)}, bf16[32,1024]{1,0:T(8,128)(2,1)S(1)}, u32[]{:S(2)}, u32[]{:S(2)}) collective-permute-start(bf16[32,1024]{1,0:T(8,128)(2,1)S(1)} %attend.4.refs_0_), channel_id=1, source_target_pairs={{0,2},{1,3},{2,0},{3,1},{4,6},{5,7},{6,4},{7,5},{8,10},{9,11},{10,... | collective-permute-start | bytes 196616 | tf_op jit(solution)/shard_map/ppermute | solution.py:29
  58.4 6.3 %collective-permute-start.24 = (bf16[32,1024]{1,0:T(8,128)(2,1)S(1)}, bf16[32,1024]{1,0:T(8,128)(2,1)S(1)}, u32[]{:S(2)}, u32[]{:S(2)}) collective-permute-start(bf16[32,1024]{1,0:T(8,128)(2,1)S(1)} %attend.4.refs_0_), channel_id=1, source_target_pairs={{0,4},{1,5},{2,6},{3,7},{4,0},{5,1},{6,2},{7,3},{8,12},{9,13},{10,... | collective-permute-start | bytes 196616 | tf_op jit(solution)/shard_map/ppermute | solution.py:29
  60.7 6.4 %collective-permute-start.26 = (bf16[32,1024]{1,0:T(8,128)(2,1)S(1)}, bf16[32,1024]{1,0:T(8,128)(2,1)}, u32[]{:S(2)}, u32[]{:S(2)}) collective-permute-start(bf16[32,1024]{1,0:T(8,128)(2,1)S(1)} %attend.4.refs_0_), channel_id=1, source_target_pairs={{0,6},{1,7},{2,4},{3,5},{4,2},{5,3},{6,0},{7,1},{8,14},{9,15},{10,... | collective-permute-start | bytes 196616 | tf_op jit(solution)/shard_map/ppermute | solution.py:29
  61.9 6.0 %collective-permute-start.21 = (bf16[32,1024]{1,0:T(8,128)(2,1)S(1)}, bf16[32,1024]{1,0:T(8,128)(2,1)}, u32[]{:S(2)}, u32[]{:S(2)}) collective-permute-start(bf16[32,1024]{1,0:T(8,128)(2,1)S(1)} %attend.4.refs_0_), channel_id=1, source_target_pairs={{0,1},{1,0},{2,3},{3,2},{4,5},{5,4},{6,7},{7,6},{8,9},{9,8},{10,11... | collective-permute-start | bytes 196616 | tf_op jit(solution)/shard_map/ppermute | solution.py:29
  63.1 4.8 %collective-permute-start.23 = (bf16[32,1024]{1,0:T(8,128)(2,1)S(1)}, bf16[32,1024]{1,0:T(8,128)(2,1)}, u32[]{:S(2)}, u32[]{:S(2)}) collective-permute-start(bf16[32,1024]{1,0:T(8,128)(2,1)S(1)} %collective-permute-done.22.refs_2_), channel_id=1, source_target_pairs={{0,1},{1,0},{2,3},{3,2},{4,5},{5,4},{6,7},{7,6},{8,9},{9,8},{10,11... | collective-permute-start | bytes 196616 | tf_op jit(solution)/shard_map/ppermute | solution.py:29
  85.0 5.9 %collective-permute-start.30 = (bf16[32,1024]{1,0:T(8,128)(2,1)S(1)}, bf16[32,1024]{1,0:T(8,128)(2,1)S(1)}, u32[]{:S(2)}, u32[]{:S(2)}) collective-permute-start(bf16[32,1024]{1,0:T(8,128)(2,1)S(1)} %collective-permute-done.28.refs_0_.refs_8_), channel_id=1, source_target_pairs={{0,2},{1,3},{2,0},{3,1},{4,6},{5,7},{6,4},{7,5},{8,10},{9,11},{10,... | collective-permute-start | bytes 196616 | tf_op jit(solution)/shard_map/ppermute | solution.py:29
  85.7 5.4 %collective-permute-start.32 = (bf16[32,1024]{1,0:T(8,128)(2,1)S(1)}, bf16[32,1024]{1,0:T(8,128)(2,1)S(1)}, u32[]{:S(2)}, u32[]{:S(2)}) collective-permute-start(bf16[32,1024]{1,0:T(8,128)(2,1)S(1)} %collective-permute-done.28.refs_0_.refs_8_), channel_id=1, source_target_pairs={{0,4},{1,5},{2,6},{3,7},{4,0},{5,1},{6,2},{7,3},{8,12},{9,13},{10,... | collective-permute-start | bytes 196616 | tf_op jit(solution)/shard_map/ppermute | solution.py:29
  88.2 5.9 %collective-permute-start.34 = (bf16[32,1024]{1,0:T(8,128)(2,1)S(1)}, bf16[32,1024]{1,0:T(8,128)(2,1)S(1)}, u32[]{:S(2)}, u32[]{:S(2)}) collective-permute-start(bf16[32,1024]{1,0:T(8,128)(2,1)S(1)} %collective-permute-done.28.refs_0_.refs_8_), channel_id=1, source_target_pairs={{0,6},{1,7},{2,4},{3,5},{4,2},{5,3},{6,0},{7,1},{8,14},{9,15},{10,... | collective-permute-start | bytes 196616 | tf_op jit(solution)/shard_map/ppermute | solution.py:29
  88.5 7.3 %collective-permute-start.29 = (bf16[32,1024]{1,0:T(8,128)(2,1)S(1)}, bf16[32,1024]{1,0:T(8,128)(2,1)S(1)}, u32[]{:S(2)}, u32[]{:S(2)}) collective-permute-start(bf16[32,1024]{1,0:T(8,128)(2,1)S(1)} %collective-permute-done.28.refs_0_.refs_8_), channel_id=1, source_target_pairs={{0,1},{1,0},{2,3},{3,2},{4,5},{5,4},{6,7},{7,6},{8,9},{9,8},{10,11... | collective-permute-start | bytes 196616 | tf_op jit(solution)/shard_map/ppermute | solution.py:29
  90.9 4.9 %collective-permute-start.31 = (bf16[32,1024]{1,0:T(8,128)(2,1)S(1)}, bf16[32,1024]{1,0:T(8,128)(2,1)S(1)}, u32[]{:S(2)}, u32[]{:S(2)}) collective-permute-start(bf16[32,1024]{1,0:T(8,128)(2,1)S(1)} %collective-permute-done.30.refs_2_), channel_id=1, source_target_pairs={{0,1},{1,0},{2,3},{3,2},{4,5},{5,4},{6,7},{7,6},{8,9},{9,8},{10,11... | collective-permute-start | bytes 196616 | tf_op jit(solution)/shard_map/ppermute | solution.py:29
  97.9 4.8 %collective-permute-start.37 = (bf16[16,1152]{1,0:T(8,128)(2,1)S(1)}, bf16[16,1152]{1,0:T(8,128)(2,1)S(1)}, u32[]{:S(2)}, u32[]{:S(2)}) collective-permute-start(bf16[16,1152]{1,0:T(8,128)(2,1)S(1)} %get-tuple-element.67), channel_id=1, source_target_pairs={{0,2},{1,3},{2,0},{3,1},{4,6},{5,7},{6,4},{7,5},{8,10},{9,11},{10,... | collective-permute-start | bytes 110600 | tf_op jit(solution)/shard_map/ppermute | solution.py:29
  98.0 4.7 %collective-permute-start.39 = (bf16[16,1152]{1,0:T(8,128)(2,1)S(1)}, bf16[16,1152]{1,0:T(8,128)(2,1)S(1)}, u32[]{:S(2)}, u32[]{:S(2)}) collective-permute-start(bf16[16,1152]{1,0:T(8,128)(2,1)S(1)} %get-tuple-element.68), channel_id=1, source_target_pairs={{0,4},{1,5},{2,6},{3,7},{4,0},{5,1},{6,2},{7,3},{8,12},{9,13},{10,... | collective-permute-start | bytes 110600 | tf_op jit(solution)/shard_map/ppermute | solution.py:29
  99.7 4.7 %collective-permute-start.41 = (bf16[16,1152]{1,0:T(8,128)(2,1)S(1)}, bf16[16,1152]{1,0:T(8,128)(2,1)S(1)}, u32[]{:S(2)}, u32[]{:S(2)}) collective-permute-start(bf16[16,1152]{1,0:T(8,128)(2,1)S(1)} %get-tuple-element.69), channel_id=1, source_target_pairs={{0,6},{1,7},{2,4},{3,5},{4,2},{5,3},{6,0},{7,1},{8,14},{9,15},{10,... | collective-permute-start | bytes 110600 | tf_op jit(solution)/shard_map/ppermute | solution.py:29
  101.6 14.6 %collective-permute-start.36 = (bf16[16,1152]{1,0:T(8,128)(2,1)S(1)}, bf16[16,1152]{1,0:T(8,128)(2,1)S(1)}, u32[]{:S(2)}, u32[]{:S(2)}) collective-permute-start(bf16[16,1152]{1,0:T(8,128)(2,1)S(1)} %get-tuple-element.66.refs_0_), channel_id=1, source_target_pairs={{0,1},{1,0},{2,3},{3,2},{4,5},{5,4},{6,7},{7,6},{8,9},{9,8},{10,11... | collective-permute-start | bytes 110600 | tf_op jit(solution)/shard_map/ppermute | solution.py:29
  102.8 13.4 %collective-permute-start.38 = (bf16[16,1152]{1,0:T(8,128)(2,1)S(1)}, bf16[16,1152]{1,0:T(8,128)(2,1)S(1)}, u32[]{:S(2)}, u32[]{:S(2)}) collective-permute-start(bf16[16,1152]{1,0:T(8,128)(2,1)S(1)} %collective-permute-done.37.refs_2_), channel_id=1, source_target_pairs={{0,1},{1,0},{2,3},{3,2},{4,5},{5,4},{6,7},{7,6},{8,9},{9,8},{10,11... | collective-permute-start | bytes 110600 | tf_op jit(solution)/shard_map/ppermute | solution.py:29
  102.8 13.4 %collective-permute-start.40 = (bf16[16,1152]{1,0:T(8,128)(2,1)S(1)}, bf16[16,1152]{1,0:T(8,128)(2,1)S(1)}, u32[]{:S(2)}, u32[]{:S(2)}) collective-permute-start(bf16[16,1152]{1,0:T(8,128)(2,1)S(1)} %collective-permute-done.39.refs_4_), channel_id=1, source_target_pairs={{0,1},{1,0},{2,3},{3,2},{4,5},{5,4},{6,7},{7,6},{8,9},{9,8},{10,11... | collective-permute-start | bytes 110600 | tf_op jit(solution)/shard_map/ppermute | solution.py:29
  104.5 11.7 %collective-permute-start.42 = (bf16[16,1152]{1,0:T(8,128)(2,1)S(1)}, bf16[16,1152]{1,0:T(8,128)(2,1)S(1)}, u32[]{:S(2)}, u32[]{:S(2)}) collective-permute-start(bf16[16,1152]{1,0:T(8,128)(2,1)S(1)} %collective-permute-done.41.refs_6_), channel_id=1, source_target_pairs={{0,1},{1,0},{2,3},{3,2},{4,5},{5,4},{6,7},{7,6},{8,9},{9,8},{10,11... | collective-permute-start | bytes 110600 | tf_op jit(solution)/shard_map/ppermute | solution.py:29
  120.4 4.9 %collective-permute-start.43 = (bf16[8,1280]{1,0:T(8,128)(2,1)S(1)}, bf16[8,1280]{1,0:T(8,128)(2,1)S(1)}, u32[]{:S(2)}, u32[]{:S(2)}) collective-permute-start(bf16[8,1280]{1,0:T(8,128)(2,1)S(1)} %get-tuple-element.70.refs_0_), channel_id=1, source_target_pairs={{0,1},{1,0},{2,3},{3,2},{4,5},{5,4},{6,7},{7,6},{8,9},{9,8},{10,11... | collective-permute-start | bytes 61448 | tf_op jit(solution)/shard_map/ppermute | solution.py:29
  130.8 4.8 %collective-permute-start.51 = (bf16[32,1024]{1,0:T(8,128)(2,1)S(1)}, bf16[32,1024]{1,0:T(8,128)(2,1)S(1)}, u32[]{:S(2)}, u32[]{:S(2)}) collective-permute-start(bf16[32,1024]{1,0:T(8,128)(2,1)S(1)} %attend.5.refs_0_), channel_id=1, source_target_pairs={{0,2},{1,3},{2,0},{3,1},{4,6},{5,7},{6,4},{7,5},{8,10},{9,11},{10,... | collective-permute-start | bytes 196616 | tf_op jit(solution)/shard_map/ppermute | solution.py:29
  130.9 5.5 %collective-permute-start.53 = (bf16[32,1024]{1,0:T(8,128)(2,1)S(1)}, bf16[32,1024]{1,0:T(8,128)(2,1)S(1)}, u32[]{:S(2)}, u32[]{:S(2)}) collective-permute-start(bf16[32,1024]{1,0:T(8,128)(2,1)S(1)} %attend.5.refs_0_), channel_id=1, source_target_pairs={{0,4},{1,5},{2,6},{3,7},{4,0},{5,1},{6,2},{7,3},{8,12},{9,13},{10,... | collective-permute-start | bytes 196616 | tf_op jit(solution)/shard_map/ppermute | solution.py:29
  132.4 7.5 %collective-permute-start.55 = (bf16[32,1024]{1,0:T(8,128)(2,1)S(1)}, bf16[32,1024]{1,0:T(8,128)(2,1)S(1)}, u32[]{:S(2)}, u32[]{:S(2)}) collective-permute-start(bf16[32,1024]{1,0:T(8,128)(2,1)S(1)} %attend.5.refs_0_), channel_id=1, source_target_pairs={{0,6},{1,7},{2,4},{3,5},{4,2},{5,3},{6,0},{7,1},{8,14},{9,15},{10,... | collective-permute-start | bytes 196616 | tf_op jit(solution)/shard_map/ppermute | solution.py:29
  134.5 5.5 %collective-permute-start.50 = (bf16[32,1024]{1,0:T(8,128)(2,1)S(1)}, bf16[32,1024]{1,0:T(8,128)(2,1)S(1)}, u32[]{:S(2)}, u32[]{:S(2)}) collective-permute-start(bf16[32,1024]{1,0:T(8,128)(2,1)S(1)} %attend.5.refs_0_), channel_id=1, source_target_pairs={{0,1},{1,0},{2,3},{3,2},{4,5},{5,4},{6,7},{7,6},{8,9},{9,8},{10,11... | collective-permute-start | bytes 196616 | tf_op jit(solution)/shard_map/ppermute | solution.py:29
  148.9 5.4 %collective-permute-start.59 = (bf16[32,1024]{1,0:T(8,128)(2,1)S(1)}, bf16[32,1024]{1,0:T(8,128)(2,1)S(1)}, u32[]{:S(2)}, u32[]{:S(2)}) collective-permute-start(bf16[32,1024]{1,0:T(8,128)(2,1)S(1)} %collective-permute-done.57.refs_0_.refs_8_), channel_id=1, source_target_pairs={{0,2},{1,3},{2,0},{3,1},{4,6},{5,7},{6,4},{7,5},{8,10},{9,11},{10,... | collective-permute-start | bytes 196616 | tf_op jit(solution)/shard_map/ppermute | solution.py:29
  149.1 5.4 %collective-permute-start.61 = (bf16[32,1024]{1,0:T(8,128)(2,1)S(1)}, bf16[32,1024]{1,0:T(8,128)(2,1)S(1)}, u32[]{:S(2)}, u32[]{:S(2)}) collective-permute-start(bf16[32,1024]{1,0:T(8,128)(2,1)S(1)} %collective-permute-done.57.refs_0_.refs_8_), channel_id=1, source_target_pairs={{0,4},{1,5},{2,6},{3,7},{4,0},{5,1},{6,2},{7,3},{8,12},{9,13},{10,... | collective-permute-start | bytes 196616 | tf_op jit(solution)/shard_map/ppermute | solution.py:29
  150.0 7.5 %collective-permute-start.63 = (bf16[32,1024]{1,0:T(8,128)(2,1)S(1)}, bf16[32,1024]{1,0:T(8,128)(2,1)S(1)}, u32[]{:S(2)}, u32[]{:S(2)}) collective-permute-start(bf16[32,1024]{1,0:T(8,128)(2,1)S(1)} %collective-permute-done.57.refs_0_.refs_8_), channel_id=1, source_target_pairs={{0,6},{1,7},{2,4},{3,5},{4,2},{5,3},{6,0},{7,1},{8,14},{9,15},{10,... | collective-permute-start | bytes 196616 | tf_op jit(solution)/shard_map/ppermute | solution.py:29
  152.5 5.8 %collective-permute-start.58 = (bf16[32,1024]{1,0:T(8,128)(2,1)S(1)}, bf16[32,1024]{1,0:T(8,128)(2,1)S(1)}, u32[]{:S(2)}, u32[]{:S(2)}) collective-permute-start(bf16[32,1024]{1,0:T(8,128)(2,1)S(1)} %collective-permute-done.57.refs_0_.refs_8_), channel_id=1, source_target_pairs={{0,1},{1,0},{2,3},{3,2},{4,5},{5,4},{6,7},{7,6},{8,9},{9,8},{10,11... | collective-permute-start | bytes 196616 | tf_op jit(solution)/shard_map/ppermute | solution.py:29
  160.4 4.8 %collective-permute-start.66 = (bf16[16,1152]{1,0:T(8,128)(2,1)S(1)}, bf16[16,1152]{1,0:T(8,128)(2,1)S(1)}, u32[]{:S(2)}, u32[]{:S(2)}) collective-permute-start(bf16[16,1152]{1,0:T(8,128)(2,1)S(1)} %get-tuple-element.78), channel_id=1, source_target_pairs={{0,2},{1,3},{2,0},{3,1},{4,6},{5,7},{6,4},{7,5},{8,10},{9,11},{10,... | collective-permute-start | bytes 110600 | tf_op jit(solution)/shard_map/ppermute | solution.py:29
  162.7 4.8 %collective-permute-start.70 = (bf16[16,1152]{1,0:T(8,128)(2,1)S(1)}, bf16[16,1152]{1,0:T(8,128)(2,1)S(1)}, u32[]{:S(2)}, u32[]{:S(2)}) collective-permute-start(bf16[16,1152]{1,0:T(8,128)(2,1)S(1)} %get-tuple-element.80), channel_id=1, source_target_pairs={{0,6},{1,7},{2,4},{3,5},{4,2},{5,3},{6,0},{7,1},{8,14},{9,15},{10,... | collective-permute-start | bytes 110600 | tf_op jit(solution)/shard_map/ppermute | solution.py:29
  164.0 9.5 %collective-permute-start.65 = (bf16[16,1152]{1,0:T(8,128)(2,1)S(1)}, bf16[16,1152]{1,0:T(8,128)(2,1)S(1)}, u32[]{:S(2)}, u32[]{:S(2)}) collective-permute-start(bf16[16,1152]{1,0:T(8,128)(2,1)S(1)} %get-tuple-element.77.refs_0_), channel_id=1, source_target_pairs={{0,1},{1,0},{2,3},{3,2},{4,5},{5,4},{6,7},{7,6},{8,9},{9,8},{10,11... | collective-permute-start | bytes 110600 | tf_op jit(solution)/shard_map/ppermute | solution.py:29
  165.2 8.3 %collective-permute-start.67 = (bf16[16,1152]{1,0:T(8,128)(2,1)S(1)}, bf16[16,1152]{1,0:T(8,128)(2,1)S(1)}, u32[]{:S(2)}, u32[]{:S(2)}) collective-permute-start(bf16[16,1152]{1,0:T(8,128)(2,1)S(1)} %collective-permute-done.66.refs_2_), channel_id=1, source_target_pairs={{0,1},{1,0},{2,3},{3,2},{4,5},{5,4},{6,7},{7,6},{8,9},{9,8},{10,11... | collective-permute-start | bytes 110600 | tf_op jit(solution)/shard_map/ppermute | solution.py:29
  165.5 8.0 %collective-permute-start.69 = (bf16[16,1152]{1,0:T(8,128)(2,1)S(1)}, bf16[16,1152]{1,0:T(8,128)(2,1)S(1)}, u32[]{:S(2)}, u32[]{:S(2)}) collective-permute-start(bf16[16,1152]{1,0:T(8,128)(2,1)S(1)} %collective-permute-done.68.refs_4_), channel_id=1, source_target_pairs={{0,1},{1,0},{2,3},{3,2},{4,5},{5,4},{6,7},{7,6},{8,9},{9,8},{10,11... | collective-permute-start | bytes 110600 | tf_op jit(solution)/shard_map/ppermute | solution.py:29
  167.4 6.1 %collective-permute-start.71 = (bf16[16,1152]{1,0:T(8,128)(2,1)S(1)}, bf16[16,1152]{1,0:T(8,128)(2,1)S(1)}, u32[]{:S(2)}, u32[]{:S(2)}) collective-permute-start(bf16[16,1152]{1,0:T(8,128)(2,1)S(1)} %collective-permute-done.70.refs_6_), channel_id=1, source_target_pairs={{0,1},{1,0},{2,3},{3,2},{4,5},{5,4},{6,7},{7,6},{8,9},{9,8},{10,11... | collective-permute-start | bytes 110600 | tf_op jit(solution)/shard_map/ppermute | solution.py:29
  187.6 4.8 %collective-permute-start.80 = (bf16[32,1024]{1,0:T(8,128)(2,1)S(1)}, bf16[32,1024]{1,0:T(8,128)(2,1)S(1)}, u32[]{:S(2)}, u32[]{:S(2)}) collective-permute-start(bf16[32,1024]{1,0:T(8,128)(2,1)S(1)} %attend.6.refs_0_), channel_id=1, source_target_pairs={{0,2},{1,3},{2,0},{3,1},{4,6},{5,7},{6,4},{7,5},{8,10},{9,11},{10,... | collective-permute-start | bytes 196616 | tf_op jit(solution)/shard_map/ppermute | solution.py:29
  187.6 5.6 %collective-permute-start.82 = (bf16[32,1024]{1,0:T(8,128)(2,1)S(1)}, bf16[32,1024]{1,0:T(8,128)(2,1)S(1)}, u32[]{:S(2)}, u32[]{:S(2)}) collective-permute-start(bf16[32,1024]{1,0:T(8,128)(2,1)S(1)} %attend.6.refs_0_), channel_id=1, source_target_pairs={{0,4},{1,5},{2,6},{3,7},{4,0},{5,1},{6,2},{7,3},{8,12},{9,13},{10,... | collective-permute-start | bytes 196616 | tf_op jit(solution)/shard_map/ppermute | solution.py:29
  189.8 6.0 %collective-permute-start.84 = (bf16[32,1024]{1,0:T(8,128)(2,1)S(1)}, bf16[32,1024]{1,0:T(8,128)(2,1)S(1)}, u32[]{:S(2)}, u32[]{:S(2)}) collective-permute-start(bf16[32,1024]{1,0:T(8,128)(2,1)S(1)} %attend.6.refs_0_), channel_id=1, source_target_pairs={{0,6},{1,7},{2,4},{3,5},{4,2},{5,3},{6,0},{7,1},{8,14},{9,15},{10,... | collective-permute-start | bytes 196616 | tf_op jit(solution)/shard_map/ppermute | solution.py:29
  191.2 5.7 %collective-permute-start.79 = (bf16[32,1024]{1,0:T(8,128)(2,1)S(1)}, bf16[32,1024]{1,0:T(8,128)(2,1)S(1)}, u32[]{:S(2)}, u32[]{:S(2)}) collective-permute-start(bf16[32,1024]{1,0:T(8,128)(2,1)S(1)} %attend.6.refs_0_), channel_id=1, source_target_pairs={{0,1},{1,0},{2,3},{3,2},{4,5},{5,4},{6,7},{7,6},{8,9},{9,8},{10,11... | collective-permute-start | bytes 196616 | tf_op jit(solution)/shard_map/ppermute | solution.py:29
  206.1 5.3 %collective-permute-start.88 = (bf16[32,1024]{1,0:T(8,128)(2,1)S(1)}, bf16[32,1024]{1,0:T(8,128)(2,1)S(1)}, u32[]{:S(2)}, u32[]{:S(2)}) collective-permute-start(bf16[32,1024]{1,0:T(8,128)(2,1)S(1)} %collective-permute-done.86.refs_0_.refs_8_), channel_id=1, source_target_pairs={{0,2},{1,3},{2,0},{3,1},{4,6},{5,7},{6,4},{7,5},{8,10},{9,11},{10,... | collective-permute-start | bytes 196616 | tf_op jit(solution)/shard_map/ppermute | solution.py:29
  207.0 4.8 %collective-permute-start.90 = (bf16[32,1024]{1,0:T(8,128)(2,1)S(1)}, bf16[32,1024]{1,0:T(8,128)(2,1)S(1)}, u32[]{:S(2)}, u32[]{:S(2)}) collective-permute-start(bf16[32,1024]{1,0:T(8,128)(2,1)S(1)} %collective-permute-done.86.refs_0_.refs_8_), channel_id=1, source_target_pairs={{0,4},{1,5},{2,6},{3,7},{4,0},{5,1},{6,2},{7,3},{8,12},{9,13},{10,... | collective-permute-start | bytes 196616 | tf_op jit(solution)/shard_map/ppermute | solution.py:29
  208.5 6.6 %collective-permute-start.92 = (bf16[32,1024]{1,0:T(8,128)(2,1)S(1)}, bf16[32,1024]{1,0:T(8,128)(2,1)S(1)}, u32[]{:S(2)}, u32[]{:S(2)}) collective-permute-start(bf16[32,1024]{1,0:T(8,128)(2,1)S(1)} %collective-permute-done.86.refs_0_.refs_8_), channel_id=1, source_target_pairs={{0,6},{1,7},{2,4},{3,5},{4,2},{5,3},{6,0},{7,1},{8,14},{9,15},{10,... | collective-permute-start | bytes 196616 | tf_op jit(solution)/shard_map/ppermute | solution.py:29
  209.7 6.3 %collective-permute-start.87 = (bf16[32,1024]{1,0:T(8,128)(2,1)S(1)}, bf16[32,1024]{1,0:T(8,128)(2,1)S(1)}, u32[]{:S(2)}, u32[]{:S(2)}) collective-permute-start(bf16[32,1024]{1,0:T(8,128)(2,1)S(1)} %collective-permute-done.86.refs_0_.refs_8_), channel_id=1, source_target_pairs={{0,1},{1,0},{2,3},{3,2},{4,5},{5,4},{6,7},{7,6},{8,9},{9,8},{10,11... | collective-permute-start | bytes 196616 | tf_op jit(solution)/shard_map/ppermute | solution.py:29
  218.1 4.8 %collective-permute-start.99 = (bf16[16,1152]{1,0:T(8,128)(2,1)S(1)}, bf16[16,1152]{1,0:T(8,128)(2,1)S(1)}, u32[]{:S(2)}, u32[]{:S(2)}) collective-permute-start(bf16[16,1152]{1,0:T(8,128)(2,1)S(1)} %get-tuple-element.91), channel_id=1, source_target_pairs={{0,6},{1,7},{2,4},{3,5},{4,2},{5,3},{6,0},{7,1},{8,14},{9,15},{10,... | collective-permute-start | bytes 110600 | tf_op jit(solution)/shard_map/ppermute | solution.py:29
  220.2 4.9 %collective-permute-start.97 = (bf16[16,1152]{1,0:T(8,128)(2,1)S(1)}, bf16[16,1152]{1,0:T(8,128)(2,1)S(1)}, u32[]{:S(2)}, u32[]{:S(2)}) collective-permute-start(bf16[16,1152]{1,0:T(8,128)(2,1)S(1)} %get-tuple-element.90), channel_id=1, source_target_pairs={{0,4},{1,5},{2,6},{3,7},{4,0},{5,1},{6,2},{7,3},{8,12},{9,13},{10,... | collective-permute-start | bytes 110600 | tf_op jit(solution)/shard_map/ppermute | solution.py:29
  221.8 8.5 %collective-permute-start.94 = (bf16[16,1152]{1,0:T(8,128)(2,1)S(1)}, bf16[16,1152]{1,0:T(8,128)(2,1)S(1)}, u32[]{:S(2)}, u32[]{:S(2)}) collective-permute-start(bf16[16,1152]{1,0:T(8,128)(2,1)S(1)} %get-tuple-element.88.refs_0_), channel_id=1, source_target_pairs={{0,1},{1,0},{2,3},{3,2},{4,5},{5,4},{6,7},{7,6},{8,9},{9,8},{10,11... | collective-permute-start | bytes 110600 | tf_op jit(solution)/shard_map/ppermute | solution.py:29
  223.0 7.3 %collective-permute-start.100 = (bf16[16,1152]{1,0:T(8,128)(2,1)S(1)}, bf16[16,1152]{1,0:T(8,128)(2,1)S(1)}, u32[]{:S(2)}, u32[]{:S(2)}) collective-permute-start(bf16[16,1152]{1,0:T(8,128)(2,1)S(1)} %collective-permute-done.99.refs_6_), channel_id=1, source_target_pairs={{0,1},{1,0},{2,3},{3,2},{4,5},{5,4},{6,7},{7,6},{8,9},{9,8},{10,11... | collective-permute-start | bytes 110600 | tf_op jit(solution)/shard_map/ppermute | solution.py:29
  224.3 5.9 %collective-permute-start.96 = (bf16[16,1152]{1,0:T(8,128)(2,1)S(1)}, bf16[16,1152]{1,0:T(8,128)(2,1)S(1)}, u32[]{:S(2)}, u32[]{:S(2)}) collective-permute-start(bf16[16,1152]{1,0:T(8,128)(2,1)S(1)} %collective-permute-done.95.refs_2_), channel_id=1, source_target_pairs={{0,1},{1,0},{2,3},{3,2},{4,5},{5,4},{6,7},{7,6},{8,9},{9,8},{10,11... | collective-permute-start | bytes 110600 | tf_op jit(solution)/shard_map/ppermute | solution.py:29
  225.1 5.2 %collective-permute-start.98 = (bf16[16,1152]{1,0:T(8,128)(2,1)S(1)}, bf16[16,1152]{1,0:T(8,128)(2,1)S(1)}, u32[]{:S(2)}, u32[]{:S(2)}) collective-permute-start(bf16[16,1152]{1,0:T(8,128)(2,1)S(1)} %collective-permute-done.97.refs_4_), channel_id=1, source_target_pairs={{0,1},{1,0},{2,3},{3,2},{4,5},{5,4},{6,7},{7,6},{8,9},{9,8},{10,11... | collective-permute-start | bytes 110600 | tf_op jit(solution)/shard_map/ppermute | solution.py:29
  244.3 4.8 %collective-permute-start.109 = (bf16[32,1024]{1,0:T(8,128)(2,1)S(1)}, bf16[32,1024]{1,0:T(8,128)(2,1)S(1)}, u32[]{:S(2)}, u32[]{:S(2)}) collective-permute-start(bf16[32,1024]{1,0:T(8,128)(2,1)S(1)} %attend.7.refs_0_), channel_id=1, source_target_pairs={{0,2},{1,3},{2,0},{3,1},{4,6},{5,7},{6,4},{7,5},{8,10},{9,11},{10,... | collective-permute-start | bytes 196616 | tf_op jit(solution)/shard_map/ppermute | solution.py:29
  244.4 5.6 %collective-permute-start.111 = (bf16[32,1024]{1,0:T(8,128)(2,1)S(1)}, bf16[32,1024]{1,0:T(8,128)(2,1)S(1)}, u32[]{:S(2)}, u32[]{:S(2)}) collective-permute-start(bf16[32,1024]{1,0:T(8,128)(2,1)S(1)} %attend.7.refs_0_), channel_id=1, source_target_pairs={{0,4},{1,5},{2,6},{3,7},{4,0},{5,1},{6,2},{7,3},{8,12},{9,13},{10,... | collective-permute-start | bytes 196616 | tf_op jit(solution)/shard_map/ppermute | solution.py:29
  246.5 6.1 %collective-permute-start.113 = (bf16[32,1024]{1,0:T(8,128)(2,1)S(1)}, bf16[32,1024]{1,0:T(8,128)(2,1)S(1)}, u32[]{:S(2)}, u32[]{:S(2)}) collective-permute-start(bf16[32,1024]{1,0:T(8,128)(2,1)S(1)} %attend.7.refs_0_), channel_id=1, source_target_pairs={{0,6},{1,7},{2,4},{3,5},{4,2},{5,3},{6,0},{7,1},{8,14},{9,15},{10,... | collective-permute-start | bytes 196616 | tf_op jit(solution)/shard_map/ppermute | solution.py:29
  247.9 5.7 %collective-permute-start.108 = (bf16[32,1024]{1,0:T(8,128)(2,1)S(1)}, bf16[32,1024]{1,0:T(8,128)(2,1)S(1)}, u32[]{:S(2)}, u32[]{:S(2)}) collective-permute-start(bf16[32,1024]{1,0:T(8,128)(2,1)S(1)} %attend.7.refs_0_), channel_id=1, source_target_pairs={{0,1},{1,0},{2,3},{3,2},{4,5},{5,4},{6,7},{7,6},{8,9},{9,8},{10,11... | collective-permute-start | bytes 196616 | tf_op jit(solution)/shard_map/ppermute | solution.py:29
  258.9 4.7 %collective-permute-start.116 = (bf16[8,1024]{1,0:T(8,128)(2,1)S(1)}, bf16[8,1024]{1,0:T(8,128)(2,1)S(1)}, u32[]{:S(2)}, u32[]{:S(2)}) collective-permute-start(bf16[8,1024]{1,0:T(8,128)(2,1)S(1)} %get-tuple-element.98), channel_id=1, source_target_pairs={{0,2},{1,3},{2,0},{3,1},{4,6},{5,7},{6,4},{7,5},{8,10},{9,11},{10,... | collective-permute-start | bytes 49160 | tf_op jit(solution)/shard_map/ppermute | solution.py:29
  262.5 5.0 %collective-permute-start.115 = (bf16[8,1024]{1,0:T(8,128)(2,1)S(1)}, bf16[8,1024]{1,0:T(8,128)(2,1)S(1)}, u32[]{:S(2)}, u32[]{:S(2)}) collective-permute-start(bf16[8,1024]{1,0:T(8,128)(2,1)S(1)} %get-tuple-element.97.refs_0_), channel_id=1, source_target_pairs={{0,1},{1,0},{2,3},{3,2},{4,5},{5,4},{6,7},{7,6},{8,9},{9,8},{10,11... | collective-permute-start | bytes 49160 | tf_op jit(solution)/shard_map/ppermute | solution.py:29
  (97 other events, 946.2 us)
where the time goes:
time: 272 us; the launch traced here: 269 us
  starting transfers between devices  148 us (54%)
  Pallas kernels  60.5 us (22%)
  local copies, waits for them, and re-layouts  31.7 us (12%)
  waiting for transfers between devices  27.5 us (10%)
    ppermute x119, starting transfers between devices, swapped(): return lax.ppermute(value, 'wide', [(i, i ^ bits) for i in range(count)])  143 us
    pallas_call x21, Pallas kernels, call(): pl.pallas_call(body, out_shape=outs, in_specs=[spec for _, spec in operan...  60.5 us
    unnamed x78, local copies, waits for them, and re-layouts  29.8 us
    ppermute x119, waiting for transfers between devices, swapped(): return lax.ppermute(value, 'wide', [(i, i ^ bits) for i in range(count)])  19.9 us
    ppermute x3, waiting for transfers between devices, on_device_by_head(): lax.ppermute(held, 'segment', [(s, (s + 1) % segments) for s in range(seg...  7.6 us
  transfers between devices with their start and end apart: 122, of which 28 were waited for; matrix products, arithmetic and copies ran while one was open for 0% of the time, Pallas kernels for 6%

commit v1 on v0

--- a/solution.py
+++ b/solution.py
@@ -2,6 +2,7 @@
 
 import jax
 import jax.numpy as jnp
+import numpy as np
 from jax import lax
 from jax.experimental import pallas as pl
 from jax.experimental.pallas import tpu as pltpu
@@ -29,23 +30,35 @@
     return lax.ppermute(value, "wide", [(i, i ^ bits) for i in range(count)])
 
 
-def gathered(value):
+def then(arrays, work):
+    if work is None:
+        return arrays, None
+    done = work()
+    arrays = pl.pallas_call(
+        lambda *refs: None,
+        out_shape=[jax.ShapeDtypeStruct(array.shape, array.dtype) for array in arrays],
+        in_specs=[VMEM] * len(arrays) + [pl.BlockSpec(memory_space=pl.ANY)],
+        out_specs=[VMEM] * len(arrays),
+        input_output_aliases={i: i for i in range(len(arrays))},
+        compiler_params=pltpu.CompilerParams(vmem_limit_bytes=MIB),
+        name="then",
+    )(*arrays, done)
+    return arrays, done
+
+
+def gathered(value, work=None):
     count = lax.axis_size("wide")
-    found = [None] * count
-    found[0] = value
-    found[1] = swapped(value, 1)
-    for far in range(2, count, 2):
-        found[far] = swapped(value, far)
-    for far in range(2, count, 2):
-        found[far + 1] = swapped(found[far], 1)
-    return found
-
-
-def exchanged(blocks):
-    found = []
-    for k, block in enumerate(blocks):
-        found.append(swapped(block, 2 * k) if k else block)
-    return [part for far in found for part in (far, swapped(far, 1))]
+    far = [swapped(value, k) for k in range(2, count, 2)]
+    far, done = then(far, work)
+    found = [part for one in [value, *far] for part in (one, swapped(one, 1))]
+    return found, done
+
+
+def exchanged(blocks, work=None):
+    far = [swapped(block, 2 * k) for k, block in enumerate(blocks) if k]
+    far, done = then(far, work)
+    found = [part for one in [blocks[0], *far] for part in (one, swapped(one, 1))]
+    return found, done
 
 
 def own_half(j, block):
@@ -57,7 +70,7 @@
     return pltpu.with_memory_space_constraint(weight, pltpu.VMEM)
 
 
-def call(body, out_shape, operands, scratch=(), limit=8, kept=(), name=None):
+def call(body, out_shape, operands, scratch=(), limit=8, kept=(), cost=1, name=None):
     outs = list(out_shape)
     found = pl.pallas_call(
         body,
@@ -66,9 +79,40 @@
         out_specs=[VMEM] * len(outs),
         scratch_shapes=list(scratch),
         compiler_params=pltpu.CompilerParams(vmem_limit_bytes=limit * MIB),
+        cost_estimate=pl.CostEstimate(flops=0, transcendentals=0, bytes_accessed=cost * MIB),
         name=name,
     )(*[array for array, _ in operands], *[resident(array) for array in kept])
     return [*found, *kept]
+
+
+def load_kernel(count, *refs):
+    sources, after, outs, token, sems = refs[:count], refs[count], refs[count + 1 : -2], refs[-2], refs[-1]
+    copies = [
+        pltpu.make_async_copy(source, out, sems.at[i])
+        for i, (source, out) in enumerate(zip(sources, outs, strict=True))
+    ]
+    for copy in copies:
+        copy.start()
+    token[...] = after[:8, :HD].astype(jnp.float32)
+    for copy in copies:
+        copy.wait()
+
+
+def loaded(arrays, after):
+    *found, token = pl.pallas_call(
+        functools.partial(load_kernel, len(arrays)),
+        out_shape=[pltpu.VMEM(array.shape, array.dtype) for array in arrays]
+        + [jax.ShapeDtypeStruct((8, HD), jnp.float32)],
+        in_specs=[pl.BlockSpec(memory_space=pl.ANY)] * len(arrays) + [VMEM],
+        out_specs=[VMEM] * (len(arrays) + 1),
+        scratch_shapes=[pltpu.SemaphoreType.DMA((len(arrays),))],
+        compiler_params=pltpu.CompilerParams(vmem_limit_bytes=4 * MIB),
+        cost_estimate=pl.CostEstimate(
+            flops=0, transcendentals=0, bytes_accessed=sum(array.nbytes for array in arrays)
+        ),
+        name="load",
+    )(*[pltpu.with_memory_space_constraint(array, pltpu.HBM) for array in arrays], after)
+    return found, token
 
 
 def dot(left, right):
@@ -128,10 +172,36 @@
         out[slots, query_cols:] = for_value.astype(jnp.bfloat16)
 
 
-def enter_kernel(count, own_rows, capacity, owner_ref, *refs):
+def open_kernel(hidden, names, lengths, inverse, entering, cosine, sine):
+    micro, local_rows, width = hidden.shape
+    own_rows = micro * local_rows
+    part = entering.shape[1] - HD
+    count = width // part
+    rows = jnp.concatenate([hidden[m].astype(jnp.float32) for m in range(micro)], 0)
+    entering[:, :part] = jnp.concatenate(
+        [rows[:, i * part : (i + 1) * part] for i in range(count)], 0
+    ).astype(jnp.bfloat16)
+    row = lax.broadcasted_iota(jnp.int32, (count * own_rows, HD), 0) % own_rows
+    name = jnp.zeros((count * own_rows, HD), jnp.float32)
+    for r in range(own_rows):
+        one = names[r // local_rows, r % local_rows, 0].astype(jnp.float32)
+        name = jnp.where(row == r, one, name)
+    entering[:, part:] = name.astype(jnp.bfloat16)
+    row = lax.broadcasted_iota(jnp.int32, cosine.shape, 0) % own_rows
+    position = jnp.zeros(cosine.shape, jnp.float32)
+    for r in range(own_rows):
+        one = lengths[r // local_rows, r % local_rows].astype(jnp.float32)
+        position = jnp.where(row == r, one, position)
+    angles = position * inverse[...]
+    front = lax.broadcasted_iota(jnp.int32, cosine.shape, 1) < HD // 2
+    cosine[...] = jnp.cos(angles)
+    sine[...] = jnp.where(front, -jnp.sin(angles), jnp.sin(angles))
+
+
+def enter_kernel(count, own_rows, capacity, *refs):
     chunks, rest = refs[:count], refs[count:]
     gain, down, up_query, up_value, normed, held, ident, *correction, spread = rest
-    owner = owner_ref[0]
+    owner = lax.axis_index("wide")
     rows = count * own_rows
     part = gain.shape[1] // count
     spread[...] = by_part(owner, chunks, own_rows)
@@ -151,10 +221,10 @@
     adapter_part(owner, ident, normed, down, up_query, up_value, correction, capacity)
 
 
-def norm_kernel(count, capacity, owner_ref, *refs):
+def norm_kernel(count, capacity, *refs):
     chunks, rest = refs[:count], refs[count:]
     ident, gain, down, up_query, up_value, normed, *correction = rest
-    owner = owner_ref[0]
+    owner = lax.axis_index("wide")
     rows, part = chunks[0].shape
     squares = jnp.zeros((rows, 1), jnp.float32)
     for chunk in chunks:
@@ -179,9 +249,9 @@
     out[:, wide + narrow :] = dot(normed[...], value[...])
 
 
-def correct_kernel(count, capacity, query_cols, key_cols, owner_ref, base, ident, *refs):
+def correct_kernel(count, capacity, query_cols, key_cols, base, ident, *refs):
     received, outs = refs[:count], refs[count:]
-    owner = owner_ref[0]
+    owner = lax.axis_index("wide")
     rows = base.shape[0]
     own_rows = rows // count
     slots = count * capacity
@@ -217,17 +287,19 @@
         out[...] = sorted_rows[k * 2 * own_rows : (k + 1) * 2 * own_rows, :]
 
 
-def attend_kernel(count, owner_ref, lengths, *refs):
-    arrived, (cosine, sine, keys, values, out) = refs[:count], refs[count:]
-    owner = owner_ref[0]
+def attend_kernel(count, lengths, *refs):
+    arrived, rest = refs[:count], refs[count:]
+    cosine, sine, keys, values, out, scores, weights = rest
+    owner = lax.axis_index("wide")
     own_rows, span = keys.shape[:2]
+    local_rows = lengths.shape[1]
     rows = GROUP * own_rows
     cos, sin = cosine[...], sine[...]
     row_of = lax.broadcasted_iota(jnp.int32, (rows, span), 0) % own_rows
     position = lax.broadcasted_iota(jnp.int32, (rows, span), 1)
     limit = jnp.zeros((rows, span), jnp.int32)
     for r in range(own_rows):
-        limit = jnp.where(row_of == r, lengths[r], limit)
+        limit = jnp.where(row_of == r, lengths[r // local_rows, r % local_rows], limit)
     valid = position < limit
     score_scale = HD ** (-0.5)
 
@@ -237,6 +309,7 @@
     def rounded(vectors):
         return vectors.astype(jnp.bfloat16).astype(jnp.float32)
 
+    fresh = []
     for j, ref in enumerate(arrived):
         packed = own_half(j, ref).astype(jnp.float32)
         query = jnp.concatenate([packed[:, i * HD : (i + 1) * HD] for i in range(GROUP)], 0)
@@ -247,7 +320,7 @@
         query = turned(query).astype(jnp.bfloat16)
         new_key = rounded(turned(new_key))
         lanes = pl.ds(pl.multiple_of((owner ^ j) * HD, HD), HD)
-        scores = jnp.zeros((rows, span), jnp.float32)
+        found = jnp.zeros((rows, span), jnp.float32)
         for r in range(own_rows):
             one = lax.dot_general(
                 query,
@@ -255,25 +328,34 @@
                 (((1,), (1,)), ((), ())),
                 preferred_element_type=jnp.float32,
             )
-            scores = jnp.where(row_of == r, one, scores)
-        scores = jnp.where(valid, scores * score_scale, -1e30)
+            found = jnp.where(row_of == r, one, found)
+        scores[j * rows : (j + 1) * rows, :] = jnp.where(valid, found * score_scale, -1e30)
         own = jnp.sum(query.astype(jnp.float32) * new_key, 1, keepdims=True) * score_scale
-        top = jnp.maximum(jnp.max(scores, 1, keepdims=True), own)
-        past = jnp.where(valid, jnp.exp(scores - top), 0.0)
+        fresh.append((own, new_value))
+    parts = []
+    for j, (own, new_value) in enumerate(fresh):
+        found = scores[j * rows : (j + 1) * rows, :]
+        top = jnp.maximum(jnp.max(found, 1, keepdims=True), own)
+        past = jnp.where(valid, jnp.exp(found - top), 0.0)
         own = jnp.exp(own - top)
         total = jnp.sum(past, 1, keepdims=True) + own
-        past = (past / total).astype(jnp.bfloat16)
-        mixed = rounded(own / total) * new_value
+        weights[j * rows : (j + 1) * rows, :] = (past / total).astype(jnp.bfloat16)
+        parts.append(rounded(own / total) * new_value)
+    for j, mixed in enumerate(parts):
+        lanes = pl.ds(pl.multiple_of((owner ^ j) * HD, HD), HD)
+        past = weights[j * rows : (j + 1) * rows, :]
         for r in range(own_rows):
-            weights = jnp.where(row_of == r, past, jnp.zeros_like(past))
-            mixed += dot(weights, values[r, :, lanes])
+            one = jnp.where(row_of == r, past, jnp.zeros_like(past))
+            mixed += dot(one, values[r, :, lanes])
         out[:, lanes] = mixed.astype(jnp.bfloat16)
 
 
-def leave_kernel(count, own_rows, tick, owner_ref, segment_ref, *refs):
-    chunks, (held, result, matrix, out, kept, *outs, spread, rows_ref) = refs[:count], refs[count:]
+def leave_kernel(count, own_rows, tick, *refs):
+    chunks, rest = refs[:count], refs[count:]
+    held, result = rest[0], rest[1] if tick else None
+    matrix, out, kept, *outs, spread, rows_ref = rest[2 if tick else 1 :]
     rows = count * own_rows
-    spread[...] = by_part(owner_ref[0], chunks, own_rows).astype(jnp.bfloat16)
+    spread[...] = by_part(lax.axis_index("wide"), chunks, own_rows).astype(jnp.bfloat16)
     for g in range(KVH):
         for j in range(GROUP):
             head = g * GROUP + j
@@ -285,17 +367,21 @@
         out[:, columns] = (held[:, columns].astype(jnp.float32) + product).astype(jnp.bfloat16)
 
     matmul_into(store, rows_ref, matrix, 256)
-    kept[...] = jnp.where(segment_ref[0] == tick, out[...], result[...])
+    before = result[...] if tick else jnp.zeros_like(out)
+    kept[...] = jnp.where(lax.axis_index("segment") == tick, out[...], before)
     if outs:
-        by_destination(owner_ref[0], kept[...], own_rows, outs)
-
-
-def join_kernel(count, owner_ref, *refs):
+        by_destination(lax.axis_index("wide"), kept[...], own_rows, outs)
+
+
+def join_kernel(count, *refs):
     blocks, out = refs[:count], refs[count]
     for j, block in enumerate(blocks):
         half = own_half(j, block)
         width = half.shape[1]
-        out[:, pl.ds(pl.multiple_of((owner_ref[0] ^ j) * width, width), width)] = half
+        columns = pl.ds(pl.multiple_of((lax.axis_index("wide") ^ j) * width, width), width)
+        for m in range(out.shape[1]):
+            local_rows = out.shape[2]
+            out[0, m, :, columns] = half[m * local_rows : (m + 1) * local_rows, :]
 
 
 def on_device_by_head(
@@ -314,11 +400,7 @@
     cached_values,
 ):
     segments = lax.axis_size("segment")
-    segment = lax.axis_index("segment")
     count = lax.axis_size("wide")
-    owner = lax.axis_index("wide")
-    owner_ref = owner.astype(jnp.int32).reshape(1)
-    segment_ref = segment.astype(jnp.int32).reshape(1)
     micro, local_rows, width = entering_hidden.shape
     own_rows = micro * local_rows
     rows = own_rows * count
@@ -338,13 +420,8 @@
     keys = rotated_key_cache[0].reshape(own_rows, span, -1)
     values = cached_values[0].reshape(own_rows, span, -1)
     gain = input_norm_gain
-
-    positions = lengths.reshape(-1)
     half = HD // 2
-    inverse = rope_base ** (-jnp.arange(half, dtype=jnp.float32) / half)
-    angles = positions.astype(jnp.float32)[:, None] * inverse[None, :]
-    cosine = jnp.tile(jnp.concatenate([jnp.cos(angles)] * 2, 1), (GROUP, 1))
-    sine = jnp.tile(jnp.concatenate([-jnp.sin(angles), jnp.sin(angles)], 1), (GROUP, 1))
+    inverse = np.tile(rope_base ** (-np.arange(half) / half), 2).astype(np.float32)[None]
 
     def blocks_of(slots, columns):
         return [jax.ShapeDtypeStruct((2 * slots, columns), jnp.bfloat16)] * (count // 2)
@@ -354,25 +431,35 @@
     ident_shape = jax.ShapeDtypeStruct((rows, HD), jnp.float32)
     correction_shapes = blocks_of(capacity, query_cols + key_cols)
 
-    own = entering_hidden.reshape(own_rows, count, part).transpose(1, 0, 2)
-    names = row_adapter_index.reshape(1, own_rows, 1).astype(jnp.bfloat16)
-    names = jnp.broadcast_to(names, (count, own_rows, HD))
-    entering = jnp.concatenate([own, names], 2).reshape(count * own_rows, part + HD)
-
+    angle_shape = jax.ShapeDtypeStruct((GROUP * own_rows, HD), jnp.float32)
+    entering, cosine, sine = call(
+        open_kernel,
+        [jax.ShapeDtypeStruct((rows, part + HD), jnp.bfloat16), angle_shape, angle_shape],
+        [(entering_hidden, VMEM), (row_adapter_index, SMEM), (lengths, SMEM)]
+        + [(jnp.asarray(inverse), VMEM)],
+        name="open",
+    )
     adapters = [down, up_query, up_value]
     projections = [query_weight, key_weight, value_weight]
     caches = [keys, values]
     outputs = [output_weight]
     held = ident = None
-    result = jnp.zeros((rows, part), jnp.bfloat16)
+    result = None
     blocks = []
     for tick in range(segments):
         if tick == 0:
-            chunks = gathered(entering)
+            weights = []
+
+            def load_first():
+                weights[:], token = loaded([*adapters, *projections], entering)
+                return token
+
+            chunks, _ = gathered(entering, load_first)
+            adapters, projections = weights[:3], weights[3:]
             normed, held, ident, *found = call(
                 functools.partial(enter_kernel, count, own_rows, capacity),
                 [normed_shape, held_shape, ident_shape] + correction_shapes,
-                [(owner_ref, SMEM)] + [(c, VMEM) for c in chunks] + [(gain, VMEM)],
+                [(c, VMEM) for c in chunks] + [(gain, VMEM)],
                 [pltpu.VMEM((count * rows, part + HD), jnp.float32)],
                 kept=adapters,
                 name="enter",
@@ -381,45 +468,62 @@
             held = lax.ppermute(
                 held, "segment", [(s, (s + 1) % segments) for s in range(segments)]
             )
-            chunks = gathered(held)
+            chunks, _ = gathered(held)
             normed, *found = call(
                 functools.partial(norm_kernel, count, capacity),
                 [normed_shape] + correction_shapes,
-                [(owner_ref, SMEM)] + [(c, VMEM) for c in chunks] + [(ident, VMEM), (gain, VMEM)],
+                [(c, VMEM) for c in chunks] + [(ident, VMEM), (gain, VMEM)],
                 kept=adapters,
                 name="norm",
             )
-        correction, adapters = found[: count // 2], found[count // 2 :]
-        received = exchanged(correction)
-        base, *projections = call(
-            project_kernel,
-            [jax.ShapeDtypeStruct((rows, packed_cols), jnp.float32)],
-            [(normed, VMEM)],
-            kept=projections,
-            name="project",
-        )
+        correction = found[: count // 2]
+
+        def project():
+            return call(
+                project_kernel,
+                [jax.ShapeDtypeStruct((rows, packed_cols), jnp.float32)],
+                [(normed, VMEM)],
+                kept=projections,
+                cost=16,
+                name="project",
+            )[0]
+
+        received, base = exchanged(correction, project)
         packed = call(
             functools.partial(correct_kernel, count, capacity, query_cols, key_cols),
             blocks_of(own_rows, packed_cols),
-            [(owner_ref, SMEM), (base, VMEM), (ident, VMEM)] + [(r, VMEM) for r in received],
+            [(base, VMEM), (ident, VMEM)] + [(r, VMEM) for r in received],
             name="correct",
         )
-        arrived = exchanged(packed)
-        attended, *caches = call(
+
+        def load_caches():
+            caches[:], token = loaded(caches, packed[0])
+            return token
+
+        def load_output():
+            outputs[:], token = loaded(outputs, attended)
+            return token
+
+        arrived, _ = exchanged(packed, None if tick else load_caches)
+        attended, *_ = call(
             functools.partial(attend_kernel, count),
             [jax.ShapeDtypeStruct((GROUP * own_rows, KVH * HD), jnp.bfloat16)],
-            [(owner_ref, SMEM), (positions, SMEM)] + [(a, VMEM) for a in arrived]
+            [(lengths, SMEM)] + [(a, VMEM) for a in arrived]
             + [(cosine, VMEM), (sine, VMEM)],
+            [
+                pltpu.VMEM((GROUP * rows, span), jnp.float32),
+                pltpu.VMEM((GROUP * rows, span), jnp.bfloat16),
+            ],
             kept=caches,
             name="attend",
         )
-        chunks = gathered(attended)
+        chunks, _ = gathered(attended, None if tick else load_output)
         last = tick == segments - 1
         held, result, *found = call(
             functools.partial(leave_kernel, count, own_rows, tick),
             [held_shape, held_shape] + (blocks_of(own_rows, part) if last else []),
-            [(owner_ref, SMEM), (segment_ref, SMEM)] + [(c, VMEM) for c in chunks]
-            + [(held, VMEM), (result, VMEM)],
+            [(c, VMEM) for c in chunks]
+            + [(held, VMEM)] + ([(result, VMEM)] if tick else []),
             [
                 pltpu.VMEM((GROUP * rows, KVH * HD), jnp.bfloat16),
                 pltpu.VMEM((rows, width), jnp.bfloat16),
@@ -427,14 +531,14 @@
             kept=outputs,
             name="leave",
         )
-        blocks, outputs = found[:-1], found[-1:]
+        blocks = found[:-1]
     (joined,) = call(
         functools.partial(join_kernel, count),
-        [jax.ShapeDtypeStruct((own_rows, width), jnp.bfloat16)],
-        [(owner_ref, SMEM)] + [(b, VMEM) for b in exchanged(blocks)],
+        [jax.ShapeDtypeStruct((1, micro, local_rows, width), jnp.bfloat16)],
+        [(b, VMEM) for b in exchanged(blocks)[0]],
         name="join",
     )
-    return joined.reshape(1, micro, local_rows, width)
+    return joined
 
 
 def passed_along(value, axis, steps):

time: 272 us -> 234 us (0.86)
  starting transfers between devices: 148 us -> 119 us
  local copies, waits for them, and re-layouts: 31.7 us -> 2.97 us
  waiting for transfers between devices: 27.5 us -> 39.9 us
  Pallas kernels: 60.5 us -> 68.3 us
    ppermute x119, starting transfers between devices: 143 us -> 115 us  [swapped(): return lax.ppermute(value, 'wide', [(i, i ^ bits) for i in range(count)])]
    unnamed x78 -> x19, local copies, waits for them, and re-layouts: 29.8 us -> 2.97 us
    pallas_call x0 -> x10, Pallas kernels: none -> 16.7 us  [the longest x3 16.7 us: loaded(): pl.pallas_call(functools.partial(load_kernel, len(arrays)), out_shape=[pl...]
    ppermute x119, waiting for transfers between devices: 19.9 us -> 31.7 us  [swapped(): return lax.ppermute(value, 'wide', [(i, i ^ bits) for i in range(count)])]
    pallas_call x21 -> x22, Pallas kernels: 60.5 us -> 51.6 us  [call(): pl.pallas_call(body, out_shape=outs, in_specs=[spec for _, spec in operan...]
  transfers between devices with their start and end apart: 122 -> 122, of which waited for: 28 -> 56; matrix products, arithmetic and copies ran while one was open for 0% -> 0% of each run, Pallas kernels for 6% -> 14%
where the time goes in v1:
time: 234 us; the launch traced here: 231 us
  starting transfers between devices  119 us (51%)
  Pallas kernels  68.3 us (29%)
  waiting for transfers between devices  39.9 us (17%)
  local copies, waits for them, and re-layouts  2.97 us (1%)
    ppermute x119, starting transfers between devices, swapped(): return lax.ppermute(value, 'wide', [(i, i ^ bits) for i in range(count)])  115 us
    pallas_call x22, Pallas kernels, call(): pl.pallas_call(body, out_shape=outs, in_specs=[spec for _, spec in operan...  51.6 us
    ppermute x119, waiting for transfers between devices, swapped(): return lax.ppermute(value, 'wide', [(i, i ^ bits) for i in range(count)])  31.7 us
    pallas_call x3, Pallas kernels, loaded(): pl.pallas_call(functools.partial(load_kernel, len(arrays)), out_shape=[pl...  16.7 us
    ppermute x3, waiting for transfers between devices, on_device_by_head(): lax.ppermute(held, 'segment', [(s, (s + 1) % segments) for s in range(seg...  8.18 us
  transfers between devices with their start and end apart: 122, of which 56 were waited for; matrix products, arithmetic and copies ran while one was open for 0% of the time, Pallas kernels for 14%

profile of v1, /device:TPU:7, one launch (start us, length us, event | category | flops | bytes accessed | tf_op | source)
XLA Modules:
  0.0 230.6 jit_solution(1824597041513843789)
XLA Ops:
  3.7 3.4 %collective-permute-start.3 = (bf16[32,1152]{1,0:T(8,128)(2,1)S(1)}, bf16[32,1152]{1,0:T(8,128)(2,1)S(1)}, u32[]{:S(2)}, u32[]{:S(2)}) collective-permute-start(bf16[32,1152]{1,0:T(8,128)(2,1)S(1)} %get-tuple-element.89.refs_6_.refs_0_), channel_id=1, source_target_pairs={{0,6},{1,7},{2,4},{3,5},{4,2},{5,3},{6,0},{7,1},{8,14},{9,15},{10,... | collective-permute-start | bytes 221192 | tf_op jit(solution)/shard_map/ppermute | solution.py:30
  7.4 1.4 collective-permute-start
  8.8 8.0 %load.3 = (bf16[1,8192,128]{2,1,0:T(8,128)(2,1)S(1)}, bf16[1,64,8192]{2,1,0:T(8,128)(2,1)S(1)}, bf16[1,64,1024]{2,1,0:T(8,128)(2,1)S(1)}, bf16[8192,1024]{1,0:T(...) custom-call(bf16[1,8192,128]{2,1,0:T(8,128)(2,1)} %bitcast.13, ...), custom_call_target="tpu_custom_call" | custom-call | bytes 24248320 | tf_op jit(solution)/shard_map/load/pallas_call | solution.py:102
  18.7 1.4 enter.1
  21.2 2.6 %collective-permute-start.9 = (bf16[16,1152]{1,0:T(8,128)(2,1)S(1)}, bf16[16,1152]{1,0:T(8,128)(2,1)S(1)}, u32[]{:S(2)}, u32[]{:S(2)}) collective-permute-start(bf16[16,1152]{1,0:T(8,128)(2,1)S(1)} %get-tuple-element.104), channel_id=1, source_target_pairs={{0,4},{1,5},{2,6},{3,7},{4,0},{5,1},{6,2},{7,3},{8,12},{9,13},{10,... | collective-permute-start | bytes 110600 | tf_op jit(solution)/shard_map/ppermute | solution.py:30
  24.7 4.1 %project.4.refs_3_.base = f32[32,1280]{1,0:T(8,128)S(1)} custom-call(bf16[32,8192]{1,0:T(8,128)(2,1)S(1)} %get-tuple-element.97.normed, bf16[8192,1024]{1,0:T(8,128)(2,1)S(1)} %get-tuple-element.98.query, bf16[8192,128]{1,0:T(8,128)(2,1)S(1)} %get-tuple-element.99.key, bf16[8192,128]{1,0:T(8,128)(2,1)S(1)} %get-tuple-element.100.value), custom_call_target="tpu_custom_call" | custom-call | bytes 16777216 | tf_op jit(solution)/shard_map/project/pallas_call | solution.py:75
  28.9 1.4 collective-permute-start.11
  32.3 2.6 %collective-permute-start.16 = (bf16[8,1280]{1,0:T(8,128)(2,1)S(1)}, bf16[8,1280]{1,0:T(8,128)(2,1)S(1)}, u32[]{:S(2)}, u32[]{:S(2)}) collective-permute-start(bf16[8,1280]{1,0:T(8,128)(2,1)S(1)} %get-tuple-element.111), channel_id=1, source_target_pairs={{0,4},{1,5},{2,6},{3,7},{4,0},{5,1},{6,2},{7,3},{8,12},{9,13},{10,... | collective-permute-start | bytes 61448 | tf_op jit(solution)/shard_map/ppermute | solution.py:30
  37.0 2.9 %load.4 = (bf16[4,384,1024]{2,1,0:T(8,128)(2,1)S(1)}, bf16[4,384,1024]{2,1,0:T(8,128)(2,1)S(1)}, f32[8,128]{1,0:T(8,128)S(1)}) custom-call(bf16[4,384,1024]{2,1,0:T(8,128)(2,1)} %bitcast.11, bf16[4,384,1024]{2,1,0:T(8,128)(2,1)} %bitcast.12, bf16[8,1280]{1,0:T(8,128)(2,1)S(1)} %get-tuple-element.109.refs_2_.refs_0_), custom_call_target="tpu_custom_call" | custom-call | bytes 6291456 | tf_op jit(solution)/shard_map/load/pallas_call | solution.py:102
  42.6 2.7 %attend.4.refs_1_.refs_0_ = bf16[32,1024]{1,0:T(8,128)(2,1)S(1)} custom-call(s32[2,2]{1,0:T(2,128)S(1)} %copy-done.7, bf16[8,1280]{1,0:T(8,128)(2,1)S(1)} %get-tuple-element.109.refs_2_.refs_0_, bf16[8,1280]{1,0:T(8,128)(2,1)S(1)} %collective-permute-done.14.refs_1_, bf16[8,1280]{1,0:T(8,128)(2,1)S(1)} %get-tuple-element.114.refs_2_, ...), custom_call_target="tpu_custom_call" | custom-call | bytes 1048576 | tf_op jit(solution)/shard_map/attend/pallas_call | solution.py:75
  46.6 2.3 collective-permute-start.22
  50.1 5.8 %load.5 = (bf16[8192,1024]{1,0:T(8,128)(2,1)S(1)}, f32[8,128]{1,0:T(8,128)S(1)}) custom-call(bf16[8192,1024]{1,0:T(8,128)(2,1)} %bitcast.10, bf16[32,1024]{1,0:T(8,128)(2,1)S(1)} %attend.4.refs_1_.refs_0_), custom_call_target="tpu_custom_call" | custom-call | bytes 16777216 | tf_op jit(solution)/shard_map/load/pallas_call | solution.py:102
  57.7 3.8 %leave.4 = (bf16[32,1024]{1,0:T(8,128)(2,1)S(1)}, bf16[32,1024]{1,0:T(8,128)(2,1)S(1)}) custom-call(bf16[32,1024]{1,0:T(8,128)(2,1)S(1)} %attend.4.refs_1_.refs_0_, bf16[32,1024]{1,0:T(8,128)(2,1)S(1)} %collective-permute-done.21.refs_1_, bf16[32,1024]{1,0:T(8,128)(2,1)S(1)} %get-tuple-element.122.refs_2_, ...), custom_call_target="tpu_custom_call" | custom-call | bytes 1048576 | tf_op jit(solution)/shard_map/leave/pallas_call | solution.py:75
  62.0 3.4 %collective-permute-done.28.refs_0_.refs_8_ = bf16[32,1024]{1,0:T(8,128)(2,1)S(1)} collective-permute-done((bf16[32,1024]{1,0:T(8,128)(2,1)S(1)}, bf16[32,1024]{1,0:T(8,128)(2,1)S(1)}, u32[]{:S(2)}, u32[]{:S(2)}) %collective-permute-start.28) | collective-permute-done | bytes 65568 | tf_op jit(solution)/shard_map/ppermute | solution.py:468
  66.4 2.4 %collective-permute-start.30 = (bf16[32,1024]{1,0:T(8,128)(2,1)S(1)}, bf16[32,1024]{1,0:T(8,128)(2,1)S(1)}, u32[]{:S(2)}, u32[]{:S(2)}) collective-permute-start(bf16[32,1024]{1,0:T(8,128)(2,1)S(1)} %collective-permute-done.28.refs_0_.refs_8_), channel_id=1, source_target_pairs={{0,2},{1,3},{2,0},{3,1},{4,6},{5,7},{6,4},{7,5},{8,10},{9,11},{10,... | collective-permute-start | bytes 196616 | tf_op jit(solution)/shard_map/ppermute | solution.py:30
  68.9 1.8 collective-permute-start.29
  70.7 2.4 %collective-permute-start.35 = (bf16[32,1024]{1,0:T(8,128)(2,1)S(1)}, bf16[32,1024]{1,0:T(8,128)(2,1)S(1)}, u32[]{:S(2)}, u32[]{:S(2)}) collective-permute-start(bf16[32,1024]{1,0:T(8,128)(2,1)S(1)} %collective-permute-done.34.refs_6_), channel_id=1, source_target_pairs={{0,1},{1,0},{2,3},{3,2},{4,5},{5,4},{6,7},{7,6},{8,9},{9,8},{10,11... | collective-permute-start | bytes 196616 | tf_op jit(solution)/shard_map/ppermute | solution.py:30
  77.0 1.4 collective-permute-start.38
  78.4 2.2 collective-permute-start.39
  80.6 4.1 %project.5.refs_3_.base = f32[32,1280]{1,0:T(8,128)S(1)} custom-call(bf16[32,8192]{1,0:T(8,128)(2,1)S(1)} %get-tuple-element.128.normed, bf16[8192,1024]{1,0:T(8,128)(2,1)S(1)} %get-tuple-element.98.query, bf16[8192,128]{1,0:T(8,128)(2,1)S(1)} %get-tuple-element.99.key, bf16[8192,128]{1,0:T(8,128)(2,1)S(1)} %copy-done.1), custom_call_target="tpu_custom_call" | custom-call | bytes 16777216 | tf_op jit(solution)/shard_map/project/pallas_call | solution.py:75
  89.5 2.2 collective-permute-start.48
  94.0 1.8 collective-permute-start.49
  96.7 2.7 %attend.5.refs_0_ = bf16[32,1024]{1,0:T(8,128)(2,1)S(1)} custom-call(s32[2,2]{1,0:T(2,128)S(1)} %copy-done.7, bf16[8,1280]{1,0:T(8,128)(2,1)S(1)} %get-tuple-element.136.refs_0_, bf16[8,1280]{1,0:T(8,128)(2,1)S(1)} %collective-permute-done.43.refs_1_, bf16[8,1280]{1,0:T(8,128)(2,1)S(1)} %collective-permute-done.44.refs_2_, ...), custom_call_target="tpu_custom_call" | custom-call | bytes 1048576 | tf_op jit(solution)/shard_map/attend/pallas_call | solution.py:75
  99.4 2.2 collective-permute-start.55
  101.6 1.4 collective-permute-start.51
  104.4 2.2 collective-permute-start.56
  106.6 1.5 collective-permute-done.53.refs_4_
  109.8 3.8 %leave.5 = (bf16[32,1024]{1,0:T(8,128)(2,1)S(1)}, bf16[32,1024]{1,0:T(8,128)(2,1)S(1)}) custom-call(bf16[32,1024]{1,0:T(8,128)(2,1)S(1)} %attend.5.refs_0_, bf16[32,1024]{1,0:T(8,128)(2,1)S(1)} %collective-permute-done.50.refs_1_, bf16[32,1024]{1,0:T(8,128)(2,1)S(1)} %collective-permute-done.51.refs_2_, ...), custom_call_target="tpu_custom_call" | custom-call | bytes 1048576 | tf_op jit(solution)/shard_map/leave/pallas_call | solution.py:75
  115.0 2.5 %collective-permute-done.57.refs_0_.refs_8_ = bf16[32,1024]{1,0:T(8,128)(2,1)S(1)} collective-permute-done((bf16[32,1024]{1,0:T(8,128)(2,1)S(1)}, bf16[32,1024]{1,0:T(8,128)(2,1)S(1)}, u32[]{:S(2)}, u32[]{:S(2)}) %collective-permute-start.57) | collective-permute-done | bytes 65568 | tf_op jit(solution)/shard_map/ppermute | solution.py:468
  117.5 2.2 collective-permute-start.63
  119.6 1.4 collective-permute-start.59
  121.0 1.8 collective-permute-start.58
  122.8 1.8 collective-permute-start.64
  124.6 1.7 collective-permute-done.61.refs_4_
  129.3 2.2 collective-permute-start.67
  132.9 4.1 %project.6.refs_3_.base = f32[32,1280]{1,0:T(8,128)S(1)} custom-call(bf16[32,8192]{1,0:T(8,128)(2,1)S(1)} %get-tuple-element.142.normed, bf16[8192,1024]{1,0:T(8,128)(2,1)S(1)} %get-tuple-element.98.query, bf16[8192,128]{1,0:T(8,128)(2,1)S(1)} %get-tuple-element.99.key, bf16[8192,128]{1,0:T(8,128)(2,1)S(1)} %copy-done.2), custom_call_target="tpu_custom_call" | custom-call | bytes 16777216 | tf_op jit(solution)/shard_map/project/pallas_call | solution.py:75
  140.5 2.2 collective-permute-start.75
  145.6 1.6 collective-permute-done.77.refs_6_
  147.2 1.9 collective-permute-start.78
  149.9 2.7 %attend.6.refs_0_ = bf16[32,1024]{1,0:T(8,128)(2,1)S(1)} custom-call(s32[2,2]{1,0:T(2,128)S(1)} %copy-done.7, bf16[8,1280]{1,0:T(8,128)(2,1)S(1)} %get-tuple-element.150.refs_0_, bf16[8,1280]{1,0:T(8,128)(2,1)S(1)} %collective-permute-done.72.refs_1_, bf16[8,1280]{1,0:T(8,128)(2,1)S(1)} %collective-permute-done.73.refs_2_, ...), custom_call_target="tpu_custom_call" | custom-call | bytes 1048576 | tf_op jit(solution)/shard_map/attend/pallas_call | solution.py:75
  153.9 2.3 collective-permute-start.80
  157.6 2.1 collective-permute-start.85
  159.8 1.5 collective-permute-done.82.refs_4_
  163.0 3.8 %leave.6 = (bf16[32,1024]{1,0:T(8,128)(2,1)S(1)}, bf16[32,1024]{1,0:T(8,128)(2,1)S(1)}) custom-call(bf16[32,1024]{1,0:T(8,128)(2,1)S(1)} %attend.6.refs_0_, bf16[32,1024]{1,0:T(8,128)(2,1)S(1)} %collective-permute-done.79.refs_1_, bf16[32,1024]{1,0:T(8,128)(2,1)S(1)} %collective-permute-done.80.refs_2_, ...), custom_call_target="tpu_custom_call" | custom-call | bytes 1048576 | tf_op jit(solution)/shard_map/leave/pallas_call | solution.py:75
  166.8 2.3 collective-permute-start.86
  169.1 2.4 %collective-permute-done.86.refs_0_.refs_8_ = bf16[32,1024]{1,0:T(8,128)(2,1)S(1)} collective-permute-done((bf16[32,1024]{1,0:T(8,128)(2,1)S(1)}, bf16[32,1024]{1,0:T(8,128)(2,1)S(1)}, u32[]{:S(2)}, u32[]{:S(2)}) %collective-permute-start.86) | collective-permute-done | bytes 65568 | tf_op jit(solution)/shard_map/ppermute | solution.py:468
  172.8 2.3 collective-permute-start.88
  175.0 1.6 collective-permute-start.87
  176.6 2.5 %collective-permute-start.93 = (bf16[32,1024]{1,0:T(8,128)(2,1)S(1)}, bf16[32,1024]{1,0:T(8,128)(2,1)S(1)}, u32[]{:S(2)}, u32[]{:S(2)}) collective-permute-start(bf16[32,1024]{1,0:T(8,128)(2,1)S(1)} %collective-permute-done.92.refs_6_), channel_id=1, source_target_pairs={{0,1},{1,0},{2,3},{3,2},{4,5},{5,4},{6,7},{7,6},{8,9},{9,8},{10,11... | collective-permute-start | bytes 196616 | tf_op jit(solution)/shard_map/ppermute | solution.py:30
  183.2 1.6 collective-permute-start.96
  184.7 2.0 collective-permute-start.97
  186.7 4.1 %project.7.refs_3_.base = f32[32,1280]{1,0:T(8,128)S(1)} custom-call(bf16[32,8192]{1,0:T(8,128)(2,1)S(1)} %get-tuple-element.156.normed, bf16[8192,1024]{1,0:T(8,128)(2,1)S(1)} %get-tuple-element.98.query, bf16[8192,128]{1,0:T(8,128)(2,1)S(1)} %get-tuple-element.99.key, bf16[8192,128]{1,0:T(8,128)(2,1)S(1)} %copy-done.3), custom_call_target="tpu_custom_call" | custom-call | bytes 16777216 | tf_op jit(solution)/shard_map/project/pallas_call | solution.py:75
  194.3 1.6 collective-permute-start.104
  195.9 2.0 collective-permute-start.106
  200.3 1.9 collective-permute-start.107
  203.0 2.7 %attend.7.refs_0_ = bf16[32,1024]{1,0:T(8,128)(2,1)S(1)} custom-call(s32[2,2]{1,0:T(2,128)S(1)} %copy-done.7, bf16[8,1280]{1,0:T(8,128)(2,1)S(1)} %get-tuple-element.164.refs_0_, bf16[8,1280]{1,0:T(8,128)(2,1)S(1)} %collective-permute-done.101.refs_1_, bf16[8,1280]{1,0:T(8,128)(2,1)S(1)} %collective-permute-done.102.refs_2_, ...), custom_call_target="tpu_custom_call" | custom-call | bytes 1048576 | tf_op jit(solution)/shard_map/attend/pallas_call | solution.py:75
  205.7 2.0 collective-permute-start.113
  207.8 1.6 collective-permute-start.109
  210.7 2.2 collective-permute-start.114
  212.9 1.5 collective-permute-done.111.refs_4_
  216.2 4.5 %leave.7 = (bf16[32,1024]{1,0:T(8,128)(2,1)}, bf16[32,1024]{1,0:T(8,128)(2,1)}, bf16[8,1024]{1,0:T(8,128)(2,1)S(1)}, bf16[8,1024]{1,0:T(8,128)(2,1)S(1)}, bf16[8...) custom-call(bf16[32,1024]{1,0:T(8,128)(2,1)S(1)} %attend.7.refs_0_, ...), custom_call_target="tpu_custom_call" | custom-call | bytes 1048576 | tf_op jit(solution)/shard_map/leave/pallas_call | solution.py:75
  220.6 2.2 collective-permute-start.118
  225.8 1.5 collective-permute-done.120.refs_6_
  227.3 1.9 collective-permute-start.121
  (231 shorter events, 72.6 us)
Async XLA Ops:
  3.7 13.2 %collective-permute-start.3 = (bf16[32,1152]{1,0:T(8,128)(2,1)S(1)}, bf16[32,1152]{1,0:T(8,128)(2,1)S(1)}, u32[]{:S(2)}, u32[]{:S(2)}) collective-permute-start(bf16[32,1152]{1,0:T(8,128)(2,1)S(1)} %get-tuple-element.89.refs_6_.refs_0_), channel_id=1, source_target_pairs={{0,6},{1,7},{2,4},{3,5},{4,2},{5,3},{6,0},{7,1},{8,14},{9,15},{10,... | collective-permute-start | bytes 221192 | tf_op jit(solution)/shard_map/ppermute | solution.py:30
  7.0 9.8 %collective-permute-start.2 = (bf16[32,1152]{1,0:T(8,128)(2,1)S(1)}, bf16[32,1152]{1,0:T(8,128)(2,1)S(1)}, u32[]{:S(2)}, u32[]{:S(2)}) collective-permute-start(bf16[32,1152]{1,0:T(8,128)(2,1)S(1)} %get-tuple-element.89.refs_6_.refs_0_), channel_id=1, source_target_pairs={{0,4},{1,5},{2,6},{3,7},{4,0},{5,1},{6,2},{7,3},{8,12},{9,13},{10,... | collective-permute-start | bytes 221192 | tf_op jit(solution)/shard_map/ppermute | solution.py:30
  7.0 9.8 %collective-permute-start.1 = (bf16[32,1152]{1,0:T(8,128)(2,1)S(1)}, bf16[32,1152]{1,0:T(8,128)(2,1)S(1)}, u32[]{:S(2)}, u32[]{:S(2)}) collective-permute-start(bf16[32,1152]{1,0:T(8,128)(2,1)S(1)} %get-tuple-element.89.refs_6_.refs_0_), channel_id=1, source_target_pairs={{0,2},{1,3},{2,0},{3,1},{4,6},{5,7},{6,4},{7,5},{8,10},{9,11},{10,... | collective-permute-start | bytes 221192 | tf_op jit(solution)/shard_map/ppermute | solution.py:30
  7.4 10.1 %collective-permute-start = (bf16[32,1152]{1,0:T(8,128)(2,1)S(1)}, bf16[32,1152]{1,0:T(8,128)(2,1)S(1)}, u32[]{:S(2)}, u32[]{:S(2)}) collective-permute-start(bf16[32,1152]{1,0:T(8,128)(2,1)S(1)} %get-tuple-element.89.refs_6_.refs_0_), channel_id=1, source_target_pairs={{0,1},{1,0},{2,3},{3,2},{4,5},{5,4},{6,7},{7,6},{8,9},{9,8},{10,11... | collective-permute-start | bytes 221192 | tf_op jit(solution)/shard_map/ppermute | solution.py:30
  20.1 8.7 %collective-permute-start.8 = (bf16[16,1152]{1,0:T(8,128)(2,1)S(1)}, bf16[16,1152]{1,0:T(8,128)(2,1)S(1)}, u32[]{:S(2)}, u32[]{:S(2)}) collective-permute-start(bf16[16,1152]{1,0:T(8,128)(2,1)S(1)} %get-tuple-element.103), channel_id=1, source_target_pairs={{0,2},{1,3},{2,0},{3,1},{4,6},{5,7},{6,4},{7,5},{8,10},{9,11},{10,... | collective-permute-start | bytes 110600 | tf_op jit(solution)/shard_map/ppermute | solution.py:30
  21.2 7.7 %collective-permute-start.9 = (bf16[16,1152]{1,0:T(8,128)(2,1)S(1)}, bf16[16,1152]{1,0:T(8,128)(2,1)S(1)}, u32[]{:S(2)}, u32[]{:S(2)}) collective-permute-start(bf16[16,1152]{1,0:T(8,128)(2,1)S(1)} %get-tuple-element.104), channel_id=1, source_target_pairs={{0,4},{1,5},{2,6},{3,7},{4,0},{5,1},{6,2},{7,3},{8,12},{9,13},{10,... | collective-permute-start | bytes 110600 | tf_op jit(solution)/shard_map/ppermute | solution.py:30
  23.8 5.1 %collective-permute-start.10 = (bf16[16,1152]{1,0:T(8,128)(2,1)S(1)}, bf16[16,1152]{1,0:T(8,128)(2,1)S(1)}, u32[]{:S(2)}, u32[]{:S(2)}) collective-permute-start(bf16[16,1152]{1,0:T(8,128)(2,1)S(1)} %get-tuple-element.105), channel_id=1, source_target_pairs={{0,6},{1,7},{2,4},{3,5},{4,2},{5,3},{6,0},{7,1},{8,14},{9,15},{10,... | collective-permute-start | bytes 110600 | tf_op jit(solution)/shard_map/ppermute | solution.py:30
  23.8 7.0 %collective-permute-start.7 = (bf16[16,1152]{1,0:T(8,128)(2,1)S(1)}, bf16[16,1152]{1,0:T(8,128)(2,1)S(1)}, u32[]{:S(2)}, u32[]{:S(2)}) collective-permute-start(bf16[16,1152]{1,0:T(8,128)(2,1)S(1)} %get-tuple-element.102.refs_0_), channel_id=1, source_target_pairs={{0,1},{1,0},{2,3},{3,2},{4,5},{5,4},{6,7},{7,6},{8,9},{9,8},{10,11... | collective-permute-start | bytes 110600 | tf_op jit(solution)/shard_map/ppermute | solution.py:30
  32.2 7.7 %collective-permute-start.15 = (bf16[8,1280]{1,0:T(8,128)(2,1)S(1)}, bf16[8,1280]{1,0:T(8,128)(2,1)S(1)}, u32[]{:S(2)}, u32[]{:S(2)}) collective-permute-start(bf16[8,1280]{1,0:T(8,128)(2,1)S(1)} %get-tuple-element.110), channel_id=1, source_target_pairs={{0,2},{1,3},{2,0},{3,1},{4,6},{5,7},{6,4},{7,5},{8,10},{9,11},{10,... | collective-permute-start | bytes 61448 | tf_op jit(solution)/shard_map/ppermute | solution.py:30
  32.3 7.6 %collective-permute-start.16 = (bf16[8,1280]{1,0:T(8,128)(2,1)S(1)}, bf16[8,1280]{1,0:T(8,128)(2,1)S(1)}, u32[]{:S(2)}, u32[]{:S(2)}) collective-permute-start(bf16[8,1280]{1,0:T(8,128)(2,1)S(1)} %get-tuple-element.111), channel_id=1, source_target_pairs={{0,4},{1,5},{2,6},{3,7},{4,0},{5,1},{6,2},{7,3},{8,12},{9,13},{10,... | collective-permute-start | bytes 61448 | tf_op jit(solution)/shard_map/ppermute | solution.py:30
  34.9 5.0 %collective-permute-start.17 = (bf16[8,1280]{1,0:T(8,128)(2,1)S(1)}, bf16[8,1280]{1,0:T(8,128)(2,1)S(1)}, u32[]{:S(2)}, u32[]{:S(2)}) collective-permute-start(bf16[8,1280]{1,0:T(8,128)(2,1)S(1)} %get-tuple-element.112), channel_id=1, source_target_pairs={{0,6},{1,7},{2,4},{3,5},{4,2},{5,3},{6,0},{7,1},{8,14},{9,15},{10,... | collective-permute-start | bytes 61448 | tf_op jit(solution)/shard_map/ppermute | solution.py:30
  35.8 5.9 %collective-permute-start.14 = (bf16[8,1280]{1,0:T(8,128)(2,1)S(1)}, bf16[8,1280]{1,0:T(8,128)(2,1)S(1)}, u32[]{:S(2)}, u32[]{:S(2)}) collective-permute-start(bf16[8,1280]{1,0:T(8,128)(2,1)S(1)} %get-tuple-element.109.refs_2_.refs_0_), channel_id=1, source_target_pairs={{0,1},{1,0},{2,3},{3,2},{4,5},{5,4},{6,7},{7,6},{8,9},{9,8},{10,11... | collective-permute-start | bytes 61448 | tf_op jit(solution)/shard_map/ppermute | solution.py:30
  45.3 10.6 %collective-permute-start.24 = (bf16[32,1024]{1,0:T(8,128)(2,1)S(1)}, bf16[32,1024]{1,0:T(8,128)(2,1)S(1)}, u32[]{:S(2)}, u32[]{:S(2)}) collective-permute-start(bf16[32,1024]{1,0:T(8,128)(2,1)S(1)} %attend.4.refs_1_.refs_0_), channel_id=1, source_target_pairs={{0,6},{1,7},{2,4},{3,5},{4,2},{5,3},{6,0},{7,1},{8,14},{9,15},{10,... | collective-permute-start | bytes 196616 | tf_op jit(solution)/shard_map/ppermute | solution.py:30
  46.6 9.2 %collective-permute-start.23 = (bf16[32,1024]{1,0:T(8,128)(2,1)S(1)}, bf16[32,1024]{1,0:T(8,128)(2,1)S(1)}, u32[]{:S(2)}, u32[]{:S(2)}) collective-permute-start(bf16[32,1024]{1,0:T(8,128)(2,1)S(1)} %attend.4.refs_1_.refs_0_), channel_id=1, source_target_pairs={{0,4},{1,5},{2,6},{3,7},{4,0},{5,1},{6,2},{7,3},{8,12},{9,13},{10,... | collective-permute-start | bytes 196616 | tf_op jit(solution)/shard_map/ppermute | solution.py:30
  46.6 9.3 %collective-permute-start.22 = (bf16[32,1024]{1,0:T(8,128)(2,1)S(1)}, bf16[32,1024]{1,0:T(8,128)(2,1)S(1)}, u32[]{:S(2)}, u32[]{:S(2)}) collective-permute-start(bf16[32,1024]{1,0:T(8,128)(2,1)S(1)} %attend.4.refs_1_.refs_0_), channel_id=1, source_target_pairs={{0,2},{1,3},{2,0},{3,1},{4,6},{5,7},{6,4},{7,5},{8,10},{9,11},{10,... | collective-permute-start | bytes 196616 | tf_op jit(solution)/shard_map/ppermute | solution.py:30
  48.9 7.7 %collective-permute-start.21 = (bf16[32,1024]{1,0:T(8,128)(2,1)S(1)}, bf16[32,1024]{1,0:T(8,128)(2,1)S(1)}, u32[]{:S(2)}, u32[]{:S(2)}) collective-permute-start(bf16[32,1024]{1,0:T(8,128)(2,1)S(1)} %attend.4.refs_1_.refs_0_), channel_id=1, source_target_pairs={{0,1},{1,0},{2,3},{3,2},{4,5},{5,4},{6,7},{7,6},{8,9},{9,8},{10,11... | collective-permute-start | bytes 196616 | tf_op jit(solution)/shard_map/ppermute | solution.py:30
  65.3 5.4 %collective-permute-start.34 = (bf16[32,1024]{1,0:T(8,128)(2,1)S(1)}, bf16[32,1024]{1,0:T(8,128)(2,1)S(1)}, u32[]{:S(2)}, u32[]{:S(2)}) collective-permute-start(bf16[32,1024]{1,0:T(8,128)(2,1)S(1)} %collective-permute-done.28.refs_0_.refs_8_), channel_id=1, source_target_pairs={{0,6},{1,7},{2,4},{3,5},{4,2},{5,3},{6,0},{7,1},{8,14},{9,15},{10,... | collective-permute-start | bytes 196616 | tf_op jit(solution)/shard_map/ppermute | solution.py:30
  66.4 7.3 %collective-permute-start.32 = (bf16[32,1024]{1,0:T(8,128)(2,1)S(1)}, bf16[32,1024]{1,0:T(8,128)(2,1)S(1)}, u32[]{:S(2)}, u32[]{:S(2)}) collective-permute-start(bf16[32,1024]{1,0:T(8,128)(2,1)S(1)} %collective-permute-done.28.refs_0_.refs_8_), channel_id=1, source_target_pairs={{0,4},{1,5},{2,6},{3,7},{4,0},{5,1},{6,2},{7,3},{8,12},{9,13},{10,... | collective-permute-start | bytes 196616 | tf_op jit(solution)/shard_map/ppermute | solution.py:30
  66.4 8.0 %collective-permute-start.30 = (bf16[32,1024]{1,0:T(8,128)(2,1)S(1)}, bf16[32,1024]{1,0:T(8,128)(2,1)S(1)}, u32[]{:S(2)}, u32[]{:S(2)}) collective-permute-start(bf16[32,1024]{1,0:T(8,128)(2,1)S(1)} %collective-permute-done.28.refs_0_.refs_8_), channel_id=1, source_target_pairs={{0,2},{1,3},{2,0},{3,1},{4,6},{5,7},{6,4},{7,5},{8,10},{9,11},{10,... | collective-permute-start | bytes 196616 | tf_op jit(solution)/shard_map/ppermute | solution.py:30
  68.9 5.6 %collective-permute-start.29 = (bf16[32,1024]{1,0:T(8,128)(2,1)S(1)}, bf16[32,1024]{1,0:T(8,128)(2,1)S(1)}, u32[]{:S(2)}, u32[]{:S(2)}) collective-permute-start(bf16[32,1024]{1,0:T(8,128)(2,1)S(1)} %collective-permute-done.28.refs_0_.refs_8_), channel_id=1, source_target_pairs={{0,1},{1,0},{2,3},{3,2},{4,5},{5,4},{6,7},{7,6},{8,9},{9,8},{10,11... | collective-permute-start | bytes 196616 | tf_op jit(solution)/shard_map/ppermute | solution.py:30
  77.0 8.8 %collective-permute-start.37 = (bf16[16,1152]{1,0:T(8,128)(2,1)S(1)}, bf16[16,1152]{1,0:T(8,128)(2,1)S(1)}, u32[]{:S(2)}, u32[]{:S(2)}) collective-permute-start(bf16[16,1152]{1,0:T(8,128)(2,1)S(1)} %get-tuple-element.130), channel_id=1, source_target_pairs={{0,2},{1,3},{2,0},{3,1},{4,6},{5,7},{6,4},{7,5},{8,10},{9,11},{10,... | collective-permute-start | bytes 110600 | tf_op jit(solution)/shard_map/ppermute | solution.py:30
  77.0 8.7 %collective-permute-start.38 = (bf16[16,1152]{1,0:T(8,128)(2,1)S(1)}, bf16[16,1152]{1,0:T(8,128)(2,1)S(1)}, u32[]{:S(2)}, u32[]{:S(2)}) collective-permute-start(bf16[16,1152]{1,0:T(8,128)(2,1)S(1)} %get-tuple-element.131), channel_id=1, source_target_pairs={{0,4},{1,5},{2,6},{3,7},{4,0},{5,1},{6,2},{7,3},{8,12},{9,13},{10,... | collective-permute-start | bytes 110600 | tf_op jit(solution)/shard_map/ppermute | solution.py:30
  78.4 7.3 %collective-permute-start.39 = (bf16[16,1152]{1,0:T(8,128)(2,1)S(1)}, bf16[16,1152]{1,0:T(8,128)(2,1)S(1)}, u32[]{:S(2)}, u32[]{:S(2)}) collective-permute-start(bf16[16,1152]{1,0:T(8,128)(2,1)S(1)} %get-tuple-element.132), channel_id=1, source_target_pairs={{0,6},{1,7},{2,4},{3,5},{4,2},{5,3},{6,0},{7,1},{8,14},{9,15},{10,... | collective-permute-start | bytes 110600 | tf_op jit(solution)/shard_map/ppermute | solution.py:30
  88.1 4.6 %collective-permute-start.44 = (bf16[8,1280]{1,0:T(8,128)(2,1)S(1)}, bf16[8,1280]{1,0:T(8,128)(2,1)S(1)}, u32[]{:S(2)}, u32[]{:S(2)}) collective-permute-start(bf16[8,1280]{1,0:T(8,128)(2,1)S(1)} %get-tuple-element.137), channel_id=1, source_target_pairs={{0,2},{1,3},{2,0},{3,1},{4,6},{5,7},{6,4},{7,5},{8,10},{9,11},{10,... | collective-permute-start | bytes 61448 | tf_op jit(solution)/shard_map/ppermute | solution.py:30
  88.2 4.5 %collective-permute-start.46 = (bf16[8,1280]{1,0:T(8,128)(2,1)S(1)}, bf16[8,1280]{1,0:T(8,128)(2,1)S(1)}, u32[]{:S(2)}, u32[]{:S(2)}) collective-permute-start(bf16[8,1280]{1,0:T(8,128)(2,1)S(1)} %get-tuple-element.138), channel_id=1, source_target_pairs={{0,4},{1,5},{2,6},{3,7},{4,0},{5,1},{6,2},{7,3},{8,12},{9,13},{10,... | collective-permute-start | bytes 61448 | tf_op jit(solution)/shard_map/ppermute | solution.py:30
  89.5 4.5 %collective-permute-start.48 = (bf16[8,1280]{1,0:T(8,128)(2,1)S(1)}, bf16[8,1280]{1,0:T(8,128)(2,1)S(1)}, u32[]{:S(2)}, u32[]{:S(2)}) collective-permute-start(bf16[8,1280]{1,0:T(8,128)(2,1)S(1)} %get-tuple-element.139), channel_id=1, source_target_pairs={{0,6},{1,7},{2,4},{3,5},{4,2},{5,3},{6,0},{7,1},{8,14},{9,15},{10,... | collective-permute-start | bytes 61448 | tf_op jit(solution)/shard_map/ppermute | solution.py:30
  99.4 5.0 %collective-permute-start.55 = (bf16[32,1024]{1,0:T(8,128)(2,1)S(1)}, bf16[32,1024]{1,0:T(8,128)(2,1)S(1)}, u32[]{:S(2)}, u32[]{:S(2)}) collective-permute-start(bf16[32,1024]{1,0:T(8,128)(2,1)S(1)} %attend.5.refs_0_), channel_id=1, source_target_pairs={{0,6},{1,7},{2,4},{3,5},{4,2},{5,3},{6,0},{7,1},{8,14},{9,15},{10,... | collective-permute-start | bytes 196616 | tf_op jit(solution)/shard_map/ppermute | solution.py:30
  101.6 6.5 %collective-permute-start.53 = (bf16[32,1024]{1,0:T(8,128)(2,1)S(1)}, bf16[32,1024]{1,0:T(8,128)(2,1)S(1)}, u32[]{:S(2)}, u32[]{:S(2)}) collective-permute-start(bf16[32,1024]{1,0:T(8,128)(2,1)S(1)} %attend.5.refs_0_), channel_id=1, source_target_pairs={{0,4},{1,5},{2,6},{3,7},{4,0},{5,1},{6,2},{7,3},{8,12},{9,13},{10,... | collective-permute-start | bytes 196616 | tf_op jit(solution)/shard_map/ppermute | solution.py:30
  101.6 7.0 %collective-permute-start.51 = (bf16[32,1024]{1,0:T(8,128)(2,1)S(1)}, bf16[32,1024]{1,0:T(8,128)(2,1)S(1)}, u32[]{:S(2)}, u32[]{:S(2)}) collective-permute-start(bf16[32,1024]{1,0:T(8,128)(2,1)S(1)} %attend.5.refs_0_), channel_id=1, source_target_pairs={{0,2},{1,3},{2,0},{3,1},{4,6},{5,7},{6,4},{7,5},{8,10},{9,11},{10,... | collective-permute-start | bytes 196616 | tf_op jit(solution)/shard_map/ppermute | solution.py:30
  103.0 5.6 %collective-permute-start.50 = (bf16[32,1024]{1,0:T(8,128)(2,1)S(1)}, bf16[32,1024]{1,0:T(8,128)(2,1)S(1)}, u32[]{:S(2)}, u32[]{:S(2)}) collective-permute-start(bf16[32,1024]{1,0:T(8,128)(2,1)S(1)} %attend.5.refs_0_), channel_id=1, source_target_pairs={{0,1},{1,0},{2,3},{3,2},{4,5},{5,4},{6,7},{7,6},{8,9},{9,8},{10,11... | collective-permute-start | bytes 196616 | tf_op jit(solution)/shard_map/ppermute | solution.py:30
  117.5 5.4 %collective-permute-start.63 = (bf16[32,1024]{1,0:T(8,128)(2,1)S(1)}, bf16[32,1024]{1,0:T(8,128)(2,1)S(1)}, u32[]{:S(2)}, u32[]{:S(2)}) collective-permute-start(bf16[32,1024]{1,0:T(8,128)(2,1)S(1)} %collective-permute-done.57.refs_0_.refs_8_), channel_id=1, source_target_pairs={{0,6},{1,7},{2,4},{3,5},{4,2},{5,3},{6,0},{7,1},{8,14},{9,15},{10,... | collective-permute-start | bytes 196616 | tf_op jit(solution)/shard_map/ppermute | solution.py:30
  119.6 6.6 %collective-permute-start.61 = (bf16[32,1024]{1,0:T(8,128)(2,1)S(1)}, bf16[32,1024]{1,0:T(8,128)(2,1)S(1)}, u32[]{:S(2)}, u32[]{:S(2)}) collective-permute-start(bf16[32,1024]{1,0:T(8,128)(2,1)S(1)} %collective-permute-done.57.refs_0_.refs_8_), channel_id=1, source_target_pairs={{0,4},{1,5},{2,6},{3,7},{4,0},{5,1},{6,2},{7,3},{8,12},{9,13},{10,... | collective-permute-start | bytes 196616 | tf_op jit(solution)/shard_map/ppermute | solution.py:30
  119.6 7.1 %collective-permute-start.59 = (bf16[32,1024]{1,0:T(8,128)(2,1)S(1)}, bf16[32,1024]{1,0:T(8,128)(2,1)S(1)}, u32[]{:S(2)}, u32[]{:S(2)}) collective-permute-start(bf16[32,1024]{1,0:T(8,128)(2,1)S(1)} %collective-permute-done.57.refs_0_.refs_8_), channel_id=1, source_target_pairs={{0,2},{1,3},{2,0},{3,1},{4,6},{5,7},{6,4},{7,5},{8,10},{9,11},{10,... | collective-permute-start | bytes 196616 | tf_op jit(solution)/shard_map/ppermute | solution.py:30
  121.0 5.8 %collective-permute-start.58 = (bf16[32,1024]{1,0:T(8,128)(2,1)S(1)}, bf16[32,1024]{1,0:T(8,128)(2,1)S(1)}, u32[]{:S(2)}, u32[]{:S(2)}) collective-permute-start(bf16[32,1024]{1,0:T(8,128)(2,1)S(1)} %collective-permute-done.57.refs_0_.refs_8_), channel_id=1, source_target_pairs={{0,1},{1,0},{2,3},{3,2},{4,5},{5,4},{6,7},{7,6},{8,9},{9,8},{10,11... | collective-permute-start | bytes 196616 | tf_op jit(solution)/shard_map/ppermute | solution.py:30
  129.3 8.8 %collective-permute-start.66 = (bf16[16,1152]{1,0:T(8,128)(2,1)S(1)}, bf16[16,1152]{1,0:T(8,128)(2,1)S(1)}, u32[]{:S(2)}, u32[]{:S(2)}) collective-permute-start(bf16[16,1152]{1,0:T(8,128)(2,1)S(1)} %get-tuple-element.144), channel_id=1, source_target_pairs={{0,2},{1,3},{2,0},{3,1},{4,6},{5,7},{6,4},{7,5},{8,10},{9,11},{10,... | collective-permute-start | bytes 110600 | tf_op jit(solution)/shard_map/ppermute | solution.py:30
  129.3 8.7 %collective-permute-start.67 = (bf16[16,1152]{1,0:T(8,128)(2,1)S(1)}, bf16[16,1152]{1,0:T(8,128)(2,1)S(1)}, u32[]{:S(2)}, u32[]{:S(2)}) collective-permute-start(bf16[16,1152]{1,0:T(8,128)(2,1)S(1)} %get-tuple-element.145), channel_id=1, source_target_pairs={{0,4},{1,5},{2,6},{3,7},{4,0},{5,1},{6,2},{7,3},{8,12},{9,13},{10,... | collective-permute-start | bytes 110600 | tf_op jit(solution)/shard_map/ppermute | solution.py:30
  131.6 6.5 %collective-permute-start.68 = (bf16[16,1152]{1,0:T(8,128)(2,1)S(1)}, bf16[16,1152]{1,0:T(8,128)(2,1)S(1)}, u32[]{:S(2)}, u32[]{:S(2)}) collective-permute-start(bf16[16,1152]{1,0:T(8,128)(2,1)S(1)} %get-tuple-element.146), channel_id=1, source_target_pairs={{0,6},{1,7},{2,4},{3,5},{4,2},{5,3},{6,0},{7,1},{8,14},{9,15},{10,... | collective-permute-start | bytes 110600 | tf_op jit(solution)/shard_map/ppermute | solution.py:30
  140.4 4.6 %collective-permute-start.73 = (bf16[8,1280]{1,0:T(8,128)(2,1)S(1)}, bf16[8,1280]{1,0:T(8,128)(2,1)S(1)}, u32[]{:S(2)}, u32[]{:S(2)}) collective-permute-start(bf16[8,1280]{1,0:T(8,128)(2,1)S(1)} %get-tuple-element.151), channel_id=1, source_target_pairs={{0,2},{1,3},{2,0},{3,1},{4,6},{5,7},{6,4},{7,5},{8,10},{9,11},{10,... | collective-permute-start | bytes 61448 | tf_op jit(solution)/shard_map/ppermute | solution.py:30
  140.5 4.5 %collective-permute-start.75 = (bf16[8,1280]{1,0:T(8,128)(2,1)S(1)}, bf16[8,1280]{1,0:T(8,128)(2,1)S(1)}, u32[]{:S(2)}, u32[]{:S(2)}) collective-permute-start(bf16[8,1280]{1,0:T(8,128)(2,1)S(1)} %get-tuple-element.152), channel_id=1, source_target_pairs={{0,4},{1,5},{2,6},{3,7},{4,0},{5,1},{6,2},{7,3},{8,12},{9,13},{10,... | collective-permute-start | bytes 61448 | tf_op jit(solution)/shard_map/ppermute | solution.py:30
  142.7 4.4 %collective-permute-start.77 = (bf16[8,1280]{1,0:T(8,128)(2,1)S(1)}, bf16[8,1280]{1,0:T(8,128)(2,1)S(1)}, u32[]{:S(2)}, u32[]{:S(2)}) collective-permute-start(bf16[8,1280]{1,0:T(8,128)(2,1)S(1)} %get-tuple-element.153), channel_id=1, source_target_pairs={{0,6},{1,7},{2,4},{3,5},{4,2},{5,3},{6,0},{7,1},{8,14},{9,15},{10,... | collective-permute-start | bytes 61448 | tf_op jit(solution)/shard_map/ppermute | solution.py:30
  144.0 5.0 %collective-permute-start.72 = (bf16[8,1280]{1,0:T(8,128)(2,1)S(1)}, bf16[8,1280]{1,0:T(8,128)(2,1)S(1)}, u32[]{:S(2)}, u32[]{:S(2)}) collective-permute-start(bf16[8,1280]{1,0:T(8,128)(2,1)S(1)} %get-tuple-element.150.refs_0_), channel_id=1, source_target_pairs={{0,1},{1,0},{2,3},{3,2},{4,5},{5,4},{6,7},{7,6},{8,9},{9,8},{10,11... | collective-permute-start | bytes 61448 | tf_op jit(solution)/shard_map/ppermute | solution.py:30
  152.6 5.1 %collective-permute-start.84 = (bf16[32,1024]{1,0:T(8,128)(2,1)S(1)}, bf16[32,1024]{1,0:T(8,128)(2,1)S(1)}, u32[]{:S(2)}, u32[]{:S(2)}) collective-permute-start(bf16[32,1024]{1,0:T(8,128)(2,1)S(1)} %attend.6.refs_0_), channel_id=1, source_target_pairs={{0,6},{1,7},{2,4},{3,5},{4,2},{5,3},{6,0},{7,1},{8,14},{9,15},{10,... | collective-permute-start | bytes 196616 | tf_op jit(solution)/shard_map/ppermute | solution.py:30
  153.9 7.3 %collective-permute-start.82 = (bf16[32,1024]{1,0:T(8,128)(2,1)S(1)}, bf16[32,1024]{1,0:T(8,128)(2,1)S(1)}, u32[]{:S(2)}, u32[]{:S(2)}) collective-permute-start(bf16[32,1024]{1,0:T(8,128)(2,1)S(1)} %attend.6.refs_0_), channel_id=1, source_target_pairs={{0,4},{1,5},{2,6},{3,7},{4,0},{5,1},{6,2},{7,3},{8,12},{9,13},{10,... | collective-permute-start | bytes 196616 | tf_op jit(solution)/shard_map/ppermute | solution.py:30
  153.9 7.8 %collective-permute-start.80 = (bf16[32,1024]{1,0:T(8,128)(2,1)S(1)}, bf16[32,1024]{1,0:T(8,128)(2,1)S(1)}, u32[]{:S(2)}, u32[]{:S(2)}) collective-permute-start(bf16[32,1024]{1,0:T(8,128)(2,1)S(1)} %attend.6.refs_0_), channel_id=1, source_target_pairs={{0,2},{1,3},{2,0},{3,1},{4,6},{5,7},{6,4},{7,5},{8,10},{9,11},{10,... | collective-permute-start | bytes 196616 | tf_op jit(solution)/shard_map/ppermute | solution.py:30
  156.2 5.6 %collective-permute-start.79 = (bf16[32,1024]{1,0:T(8,128)(2,1)S(1)}, bf16[32,1024]{1,0:T(8,128)(2,1)S(1)}, u32[]{:S(2)}, u32[]{:S(2)}) collective-permute-start(bf16[32,1024]{1,0:T(8,128)(2,1)S(1)} %attend.6.refs_0_), channel_id=1, source_target_pairs={{0,1},{1,0},{2,3},{3,2},{4,5},{5,4},{6,7},{7,6},{8,9},{9,8},{10,11... | collective-permute-start | bytes 196616 | tf_op jit(solution)/shard_map/ppermute | solution.py:30
  166.8 4.7 %collective-permute-start.86 = (bf16[32,1024]{1,0:T(8,128)(2,1)S(1)}, bf16[32,1024]{1,0:T(8,128)(2,1)S(1)}, u32[]{:S(2)}, u32[]{:S(2)}) collective-permute-start(bf16[32,1024]{1,0:T(8,128)(2,1)S(1)} %get-tuple-element.155), channel_id=1, source_target_pairs={{0,8},{8,16},{16,24},{24,0},{1,9},{9,17},{17,25},{25,1},{2,10},{10... | collective-permute-start | bytes 196616 | tf_op jit(solution)/shard_map/ppermute | solution.py:468
  171.5 5.1 %collective-permute-start.92 = (bf16[32,1024]{1,0:T(8,128)(2,1)S(1)}, bf16[32,1024]{1,0:T(8,128)(2,1)S(1)}, u32[]{:S(2)}, u32[]{:S(2)}) collective-permute-start(bf16[32,1024]{1,0:T(8,128)(2,1)S(1)} %collective-permute-done.86.refs_0_.refs_8_), channel_id=1, source_target_pairs={{0,6},{1,7},{2,4},{3,5},{4,2},{5,3},{6,0},{7,1},{8,14},{9,15},{10,... | collective-permute-start | bytes 196616 | tf_op jit(solution)/shard_map/ppermute | solution.py:30
  172.8 7.3 %collective-permute-start.90 = (bf16[32,1024]{1,0:T(8,128)(2,1)S(1)}, bf16[32,1024]{1,0:T(8,128)(2,1)S(1)}, u32[]{:S(2)}, u32[]{:S(2)}) collective-permute-start(bf16[32,1024]{1,0:T(8,128)(2,1)S(1)} %collective-permute-done.86.refs_0_.refs_8_), channel_id=1, source_target_pairs={{0,4},{1,5},{2,6},{3,7},{4,0},{5,1},{6,2},{7,3},{8,12},{9,13},{10,... | collective-permute-start | bytes 196616 | tf_op jit(solution)/shard_map/ppermute | solution.py:30
  172.8 7.8 %collective-permute-start.88 = (bf16[32,1024]{1,0:T(8,128)(2,1)S(1)}, bf16[32,1024]{1,0:T(8,128)(2,1)S(1)}, u32[]{:S(2)}, u32[]{:S(2)}) collective-permute-start(bf16[32,1024]{1,0:T(8,128)(2,1)S(1)} %collective-permute-done.86.refs_0_.refs_8_), channel_id=1, source_target_pairs={{0,2},{1,3},{2,0},{3,1},{4,6},{5,7},{6,4},{7,5},{8,10},{9,11},{10,... | collective-permute-start | bytes 196616 | tf_op jit(solution)/shard_map/ppermute | solution.py:30
  175.0 5.6 %collective-permute-start.87 = (bf16[32,1024]{1,0:T(8,128)(2,1)S(1)}, bf16[32,1024]{1,0:T(8,128)(2,1)S(1)}, u32[]{:S(2)}, u32[]{:S(2)}) collective-permute-start(bf16[32,1024]{1,0:T(8,128)(2,1)S(1)} %collective-permute-done.86.refs_0_.refs_8_), channel_id=1, source_target_pairs={{0,1},{1,0},{2,3},{3,2},{4,5},{5,4},{6,7},{7,6},{8,9},{9,8},{10,11... | collective-permute-start | bytes 196616 | tf_op jit(solution)/shard_map/ppermute | solution.py:30
  183.1 8.8 %collective-permute-start.95 = (bf16[16,1152]{1,0:T(8,128)(2,1)S(1)}, bf16[16,1152]{1,0:T(8,128)(2,1)S(1)}, u32[]{:S(2)}, u32[]{:S(2)}) collective-permute-start(bf16[16,1152]{1,0:T(8,128)(2,1)S(1)} %get-tuple-element.158), channel_id=1, source_target_pairs={{0,2},{1,3},{2,0},{3,1},{4,6},{5,7},{6,4},{7,5},{8,10},{9,11},{10,... | collective-permute-start | bytes 110600 | tf_op jit(solution)/shard_map/ppermute | solution.py:30
  183.2 8.7 %collective-permute-start.96 = (bf16[16,1152]{1,0:T(8,128)(2,1)S(1)}, bf16[16,1152]{1,0:T(8,128)(2,1)S(1)}, u32[]{:S(2)}, u32[]{:S(2)}) collective-permute-start(bf16[16,1152]{1,0:T(8,128)(2,1)S(1)} %get-tuple-element.159), channel_id=1, source_target_pairs={{0,4},{1,5},{2,6},{3,7},{4,0},{5,1},{6,2},{7,3},{8,12},{9,13},{10,... | collective-permute-start | bytes 110600 | tf_op jit(solution)/shard_map/ppermute | solution.py:30
  184.7 7.2 %collective-permute-start.97 = (bf16[16,1152]{1,0:T(8,128)(2,1)S(1)}, bf16[16,1152]{1,0:T(8,128)(2,1)S(1)}, u32[]{:S(2)}, u32[]{:S(2)}) collective-permute-start(bf16[16,1152]{1,0:T(8,128)(2,1)S(1)} %get-tuple-element.160), channel_id=1, source_target_pairs={{0,6},{1,7},{2,4},{3,5},{4,2},{5,3},{6,0},{7,1},{8,14},{9,15},{10,... | collective-permute-start | bytes 110600 | tf_op jit(solution)/shard_map/ppermute | solution.py:30
  194.2 4.6 %collective-permute-start.102 = (bf16[8,1280]{1,0:T(8,128)(2,1)S(1)}, bf16[8,1280]{1,0:T(8,128)(2,1)S(1)}, u32[]{:S(2)}, u32[]{:S(2)}) collective-permute-start(bf16[8,1280]{1,0:T(8,128)(2,1)S(1)} %get-tuple-element.165), channel_id=1, source_target_pairs={{0,2},{1,3},{2,0},{3,1},{4,6},{5,7},{6,4},{7,5},{8,10},{9,11},{10,... | collective-permute-start | bytes 61448 | tf_op jit(solution)/shard_map/ppermute | solution.py:30
  194.3 4.5 %collective-permute-start.104 = (bf16[8,1280]{1,0:T(8,128)(2,1)S(1)}, bf16[8,1280]{1,0:T(8,128)(2,1)S(1)}, u32[]{:S(2)}, u32[]{:S(2)}) collective-permute-start(bf16[8,1280]{1,0:T(8,128)(2,1)S(1)} %get-tuple-element.166), channel_id=1, source_target_pairs={{0,4},{1,5},{2,6},{3,7},{4,0},{5,1},{6,2},{7,3},{8,12},{9,13},{10,... | collective-permute-start | bytes 61448 | tf_op jit(solution)/shard_map/ppermute | solution.py:30
  195.9 4.4 %collective-permute-start.106 = (bf16[8,1280]{1,0:T(8,128)(2,1)S(1)}, bf16[8,1280]{1,0:T(8,128)(2,1)S(1)}, u32[]{:S(2)}, u32[]{:S(2)}) collective-permute-start(bf16[8,1280]{1,0:T(8,128)(2,1)S(1)} %get-tuple-element.167), channel_id=1, source_target_pairs={{0,6},{1,7},{2,4},{3,5},{4,2},{5,3},{6,0},{7,1},{8,14},{9,15},{10,... | collective-permute-start | bytes 61448 | tf_op jit(solution)/shard_map/ppermute | solution.py:30
  205.7 5.0 %collective-permute-start.113 = (bf16[32,1024]{1,0:T(8,128)(2,1)S(1)}, bf16[32,1024]{1,0:T(8,128)(2,1)S(1)}, u32[]{:S(2)}, u32[]{:S(2)}) collective-permute-start(bf16[32,1024]{1,0:T(8,128)(2,1)S(1)} %attend.7.refs_0_), channel_id=1, source_target_pairs={{0,6},{1,7},{2,4},{3,5},{4,2},{5,3},{6,0},{7,1},{8,14},{9,15},{10,... | collective-permute-start | bytes 196616 | tf_op jit(solution)/shard_map/ppermute | solution.py:30
  207.8 6.7 %collective-permute-start.111 = (bf16[32,1024]{1,0:T(8,128)(2,1)S(1)}, bf16[32,1024]{1,0:T(8,128)(2,1)S(1)}, u32[]{:S(2)}, u32[]{:S(2)}) collective-permute-start(bf16[32,1024]{1,0:T(8,128)(2,1)S(1)} %attend.7.refs_0_), channel_id=1, source_target_pairs={{0,4},{1,5},{2,6},{3,7},{4,0},{5,1},{6,2},{7,3},{8,12},{9,13},{10,... | collective-permute-start | bytes 196616 | tf_op jit(solution)/shard_map/ppermute | solution.py:30
  207.8 7.1 %collective-permute-start.109 = (bf16[32,1024]{1,0:T(8,128)(2,1)S(1)}, bf16[32,1024]{1,0:T(8,128)(2,1)S(1)}, u32[]{:S(2)}, u32[]{:S(2)}) collective-permute-start(bf16[32,1024]{1,0:T(8,128)(2,1)S(1)} %attend.7.refs_0_), channel_id=1, source_target_pairs={{0,2},{1,3},{2,0},{3,1},{4,6},{5,7},{6,4},{7,5},{8,10},{9,11},{10,... | collective-permute-start | bytes 196616 | tf_op jit(solution)/shard_map/ppermute | solution.py:30
  209.3 5.6 %collective-permute-start.108 = (bf16[32,1024]{1,0:T(8,128)(2,1)S(1)}, bf16[32,1024]{1,0:T(8,128)(2,1)S(1)}, u32[]{:S(2)}, u32[]{:S(2)}) collective-permute-start(bf16[32,1024]{1,0:T(8,128)(2,1)S(1)} %attend.7.refs_0_), channel_id=1, source_target_pairs={{0,1},{1,0},{2,3},{3,2},{4,5},{5,4},{6,7},{7,6},{8,9},{9,8},{10,11... | collective-permute-start | bytes 196616 | tf_op jit(solution)/shard_map/ppermute | solution.py:30
  220.6 4.6 %collective-permute-start.116 = (bf16[8,1024]{1,0:T(8,128)(2,1)S(1)}, bf16[8,1024]{1,0:T(8,128)(2,1)S(1)}, u32[]{:S(2)}, u32[]{:S(2)}) collective-permute-start(bf16[8,1024]{1,0:T(8,128)(2,1)S(1)} %get-tuple-element.170), channel_id=1, source_target_pairs={{0,2},{1,3},{2,0},{3,1},{4,6},{5,7},{6,4},{7,5},{8,10},{9,11},{10,... | collective-permute-start | bytes 49160 | tf_op jit(solution)/shard_map/ppermute | solution.py:30
  220.6 4.6 %collective-permute-start.118 = (bf16[8,1024]{1,0:T(8,128)(2,1)S(1)}, bf16[8,1024]{1,0:T(8,128)(2,1)S(1)}, u32[]{:S(2)}, u32[]{:S(2)}) collective-permute-start(bf16[8,1024]{1,0:T(8,128)(2,1)S(1)} %get-tuple-element.171), channel_id=1, source_target_pairs={{0,4},{1,5},{2,6},{3,7},{4,0},{5,1},{6,2},{7,3},{8,12},{9,13},{10,... | collective-permute-start | bytes 49160 | tf_op jit(solution)/shard_map/ppermute | solution.py:30
  222.9 4.4 %collective-permute-start.120 = (bf16[8,1024]{1,0:T(8,128)(2,1)S(1)}, bf16[8,1024]{1,0:T(8,128)(2,1)S(1)}, u32[]{:S(2)}, u32[]{:S(2)}) collective-permute-start(bf16[8,1024]{1,0:T(8,128)(2,1)S(1)} %get-tuple-element.172), channel_id=1, source_target_pairs={{0,6},{1,7},{2,4},{3,5},{4,2},{5,3},{6,0},{7,1},{8,14},{9,15},{10,... | collective-permute-start | bytes 49160 | tf_op jit(solution)/shard_map/ppermute | solution.py:30
  224.2 5.0 %collective-permute-start.115 = (bf16[8,1024]{1,0:T(8,128)(2,1)S(1)}, bf16[8,1024]{1,0:T(8,128)(2,1)S(1)}, u32[]{:S(2)}, u32[]{:S(2)}) collective-permute-start(bf16[8,1024]{1,0:T(8,128)(2,1)S(1)} %get-tuple-element.169.refs_0_), channel_id=1, source_target_pairs={{0,1},{1,0},{2,3},{3,2},{4,5},{5,4},{6,7},{7,6},{8,9},{9,8},{10,11... | collective-permute-start | bytes 49160 | tf_op jit(solution)/shard_map/ppermute | solution.py:30
  (67 other events, 218.8 us)
